TPU v7x, 512 devices: a whole 4x4x16 slice. The times are simulated.
512 devices in a mesh: replica: 16 (over y_lo, x, core), fsdp: 32 (over z, y_hi).
Axes of the slice: x: 4, y: 4 (y_hi: 2, y_lo: 2; y = y_hi * 2 + y_lo), z: 16, core: 2. Of those that a mesh axis runs over, the one named last changes fastest.
Arguments:
- tokens: bfloat16 [65536, 4096], P(('replica', 'fsdp')), may hold values from -6 to 6
- v_weight: bfloat16 [16, 4096, 512], P('replica', 'fsdp'), may hold values from -0.09375 to 0.09375
- out_grad: bfloat16 [65536, 512], P(('replica', 'fsdp')), may hold values from -6 to 6
- outer_params: float32 [4, 4096, 512], P(None, 'fsdp'), may hold values from -6 to 6
- momentum: float32 [4, 4096, 512], P(None, 'fsdp'), may hold values from -4 to 4
- snapshot: bfloat16 [16, 4, 4096, 512], P('replica', None, 'fsdp'), may hold values from -6 to 6
- frag_index: int32 [1], replicated, may hold values from 0 to 3
Outputs:
- values: bfloat16 [65536, 512], P(('replica', 'fsdp'))
- input_grad: bfloat16 [65536, 4096], P(('replica', 'fsdp'))
- weight_grad: bfloat16 [16, 4096, 512], P('replica', 'fsdp')
- new_outer: float32 [4, 4096, 512], P(None, 'fsdp')
- new_momentum: float32 [4, 4096, 512], P(None, 'fsdp')
All inputs are finite; a program needn't handle non-finite values.
Results may differ from a plain program's by a relative error of at most 0.001.
Values may be sent and summed in bfloat16 or wider, within the bound.
No kernel may reach another device: no remote copies, remote signals or barrier semaphores. Data moves between devices by JAX's collectives and lax.ppermute only.
A program may use at most 64 MiB of HBM per device.

v0:
```python
import math

import jax
import jax.numpy as jnp
from jax import lax
from jax.sharding import PartitionSpec as P


def body(tokens, v_weight, out_grad, outer_params, momentum, snapshot, frag_index):
    chosen = frag_index[0]
    outer_now = lax.dynamic_index_in_dim(outer_params, chosen, 0, keepdims=False)
    snap_now = lax.dynamic_index_in_dim(snapshot[0], chosen, 0, keepdims=False).astype(jnp.float32)
    summed_diff = lax.psum(outer_now - snap_now, "replica")
    pseudo_grad = summed_diff / lax.axis_size("replica")
    weight = v_weight[0]
    contract_last = (((1,), (1,)), ((), ()))
    gathered = lax.all_gather(weight, "fsdp", axis=0, tiled=True)
    values = jnp.dot(tokens, gathered, preferred_element_type=jnp.float32).astype(jnp.bfloat16)
    input_grad = lax.dot_general(
        out_grad, gathered, contract_last, preferred_element_type=jnp.float32
    ).astype(jnp.bfloat16)
    own_columns = lax.all_to_all(tokens, "fsdp", split_axis=1, concat_axis=0, tiled=True)
    contract_first = (((0,), (0,)), ((), ()))
    grad_sum = lax.dot_general(
        own_columns,
        lax.all_gather(out_grad, "fsdp", axis=0, tiled=True),
        contract_first,
        preferred_element_type=jnp.float32,
    )
    grad_scale = 1.0 / math.sqrt(tokens.shape[0] * lax.axis_size("fsdp"))
    weight_grad = (grad_sum * grad_scale).astype(jnp.bfloat16)[None]
    moment_now = lax.dynamic_index_in_dim(momentum, chosen, 0, keepdims=False)
    moment_new = 0.9 * moment_now + pseudo_grad
    outer_new = outer_now - 0.7 * (pseudo_grad + 0.9 * moment_new)
    new_momentum = lax.dynamic_update_index_in_dim(momentum, moment_new, chosen, 0)
    new_outer = lax.dynamic_update_index_in_dim(outer_params, outer_new, chosen, 0)
    return (values, input_grad, weight_grad, new_outer, new_momentum)


def solution(mesh):
    in_specs = (
        P(("replica", "fsdp"), None),
        P("replica", "fsdp", None),
        P(("replica", "fsdp"), None),
        P(None, "fsdp", None),
        P(None, "fsdp", None),
        P("replica", None, "fsdp", None),
        P(),
    )
    out_specs = (
        P(("replica", "fsdp"), None),
        P(("replica", "fsdp"), None),
        P("replica", "fsdp", None),
        P(None, "fsdp", None),
        P(None, "fsdp", None),
    )
    return jax.shard_map(body, mesh=mesh, in_specs=in_specs, out_specs=out_specs, check_vma=False)
```

profile of v0, /device:TPU:24, one launch (start us, length us, event | category | flops | bytes accessed | tf_op | source)
XLA Modules:
  0.0 373.6 jit_solution(3370537694596110420)
XLA Ops:
  8.0 0.0 copy-start.1
  8.0 0.0 all-reduce.2.cloned.1.call-start
  8.1 1.3 copy.20
  9.4 2.3 copy.21
  12.3 1.6 convert_subtract_fusion
  13.9 0.0 all-reduce.2.cloned.1.call-update
  13.9 0.0 all-gather.6.cloned.1.call-start
  14.0 0.5 all-gather.6.cloned.1.call-update
  14.5 0.0 all-gather.4.cloned.1.call-start
  14.6 0.5 all-gather.4.cloned.1.call-update
  15.1 0.0 copy-done.1
  15.1 0.0 copy-start.3
  15.1 1.3 copy.12
  16.4 18.2 %all-to-all-start = ((bf16[128,32,128]{0,2,1:T(8,128)(2,1)}), bf16[128,32,128]{0,2,1:T(8,128)(2,1)S(1)}, u32[]{:S(2)}, u32[]{:S(2)}) async-start(bf16[128,32,128]{0,2,1:T(8,128)(2,1)} %bitcast.1), calls=%async_computation | async-start | bytes 2097152 | tf_op jit(solution)/shard_map/all_to_all | solution.py:22
  34.7 117.5 %all-reduce.2.cloned.1.call-done = f32[128,512]{1,0:T(8,128)} async-done(((f32[128,512]{1,0:T(8,128)}), f32[128,512]{1,0:T(8,128)}) %all-reduce.2.cloned.1.call-update) | async-done | bytes 262160 | tf_op jit(solution)/shard_map/psum | solution.py:13
  152.2 1.1 bitcast_add_fusion
  153.3 1.8 bitcast_dynamic-update-slice_fusion
  155.2 0.0 copy-start.2
  155.2 0.0 all-to-all-done
  155.2 1.0 copy-done.2
  156.1 0.7 copy.13
  156.8 43.7 %all-gather.6.cloned.1.call-done = bf16[1,4096,512]{2,1,0:T(8,128)(2,1)} async-done(((bf16[1,128,512]{2,1,0:T(8,128)(2,1)}), bf16[1,4096,512]{2,1,0:T(8,128)(2,1)}) %all-gather.6.cloned.1.call-update) | async-done | bytes 4194320 | tf_op jit(solution)/shard_map/all_gather | solution.py:17
  200.5 0.0 copy-done.3
  200.5 0.0 copy-start
  200.5 4.8 %convolution_convert_fusion = bf16[128,4096]{1,0:T(8,128)(2,1)} fusion(bf16[128,512]{1,0:T(8,128)(2,1)S(1)} %copy-done.3, bf16[1,4096,512]{2,1,0:T(8,128)(2,1)} %all-gather.6.cloned.1.call-done), kind=kOutput, calls=%fused_computation | convolution fusion | flops 537395200 | bytes 5373952 | tf_op jit(solution)/shard_map/dot_general | solution.py:19
  205.3 0.0 copy-done
  205.3 1.4 fusion.3
  206.7 155.8 %all-gather.4.cloned.1.call-done = bf16[4096,512]{1,0:T(8,128)(2,1)} async-done(((bf16[128,512]{1,0:T(8,128)(2,1)}), bf16[4096,512]{1,0:T(8,128)(2,1)}) %all-gather.4.cloned.1.call-update) | async-done | bytes 4194320 | tf_op jit(solution)/shard_map/all_gather | solution.py:26
  362.5 3.6 fusion.7
  (1 shorter events, 0.0 us)
Async XLA Ops:
  8.0 7.1 %copy-start.1 = (bf16[128,4096]{1,0:T(8,128)(2,1)S(1)}, bf16[128,4096]{1,0:T(8,128)(2,1)}, u32[]{:S(2)}) copy-start(bf16[128,4096]{1,0:T(8,128)(2,1)} %param.7) | copy-start | bytes 3145732
  8.0 144.2 %all-reduce.2.cloned.1.call-start = ((), (), s32[]{:S(2)}) async-start(), calls=%async_computation.2 | async-start | bytes 524288 | tf_op jit(solution)/shard_map/psum | solution.py:13
  13.9 186.6 %all-gather.6.cloned.1.call-start = ((), (), s32[]{:S(2)}) async-start(), calls=%async_computation.3 | async-start | bytes 4325376 | tf_op jit(solution)/shard_map/all_gather | solution.py:17
  14.5 348.0 %all-gather.4.cloned.1.call-start = ((), (), s32[]{:S(2)}) async-start(), calls=%async_computation.1 | async-start | bytes 4325376 | tf_op jit(solution)/shard_map/all_gather | solution.py:26
  15.1 185.4 %copy-start.3 = (bf16[128,512]{1,0:T(8,128)(2,1)S(1)}, bf16[128,512]{1,0:T(8,128)(2,1)}, u32[]{:S(2)}) copy-start(bf16[128,512]{1,0:T(8,128)(2,1)} %param.9) | copy-start | bytes 393220
  16.4 138.7 %all-to-all-start = ((bf16[128,32,128]{0,2,1:T(8,128)(2,1)}), bf16[128,32,128]{0,2,1:T(8,128)(2,1)S(1)}, u32[]{:S(2)}, u32[]{:S(2)}) async-start(bf16[128,32,128]{0,2,1:T(8,128)(2,1)} %bitcast.1), calls=%async_computation | async-start | bytes 2097152 | tf_op jit(solution)/shard_map/all_to_all | solution.py:22
  155.2 1.0 copy-start.2
  200.5 4.8 %copy-start = (bf16[1,4096,512]{2,1,0:T(8,128)(2,1)S(1)}, bf16[1,4096,512]{2,1,0:T(8,128)(2,1)}, u32[]{:S(2)}) copy-start(bf16[1,4096,512]{2,1,0:T(8,128)(2,1)} %all-gather.6.cloned.1.call-done) | copy-start | bytes 12582916
Sparse Core Ops, SparseCore 0:
  14.1 138.1 all-reduce.1
Sparse Core Ops, SparseCore 1:
  17.5 182.9 all-gather.5
  203.5 159.0 all-gather.3
where the time goes:
time: 376 us; the launch traced here: 374 us
  waiting for transfers between devices  318 us (85%)
  starting transfers between devices  18.3 us (5%)
  between operations  16.2 us (4%)
  matrix products  9.76 us (3%)
  local copies, waits for them, and re-layouts  6.54 us (2%)
  other arithmetic  4.55 us (1%)
    all_gather x1, waiting for transfers between devices, body(): lax.all_gather(out_grad, 'fsdp', axis=0, tiled=True)  156 us
    psum x1, waiting for transfers between devices, body(): summed_diff = lax.psum(outer_now - snap_now, 'replica')  118 us
    all_gather x1, waiting for transfers between devices, body(): gathered = lax.all_gather(weight, 'fsdp', axis=0, tiled=True)  43.7 us
    all_to_all x1, starting transfers between devices, body(): lax.all_to_all(tokens, 'fsdp', split_axis=1, concat_axis=0, tiled=True)  18.2 us
  transfers between devices with their start and end apart: 4, of which 3 were waited for; matrix products, arithmetic and copies ran while one was open for 3% of the time, Pallas kernels for 0%

commit v1 on v0

v1 whole, which is shorter than its diff:
```python
import functools
import math

import jax
import jax.numpy as jnp
from jax import lax
from jax.experimental import pallas as pl
from jax.experimental.pallas import tpu as pltpu
from jax.sharding import Mesh
from jax.sharding import PartitionSpec as P

REPLICA = ("ylo", "x", "core")
EVERY = REPLICA + ("z", "yhi")
F32, BF16 = jnp.float32, jnp.bfloat16
VMEM = pl.BlockSpec(memory_space=pltpu.VMEM)
SMEM = pl.BlockSpec(memory_space=pltpu.SMEM)


def local(kernel, outs, name, ins):
    return pl.pallas_call(
        kernel,
        out_shape=[jax.ShapeDtypeStruct(s, d) for s, d in outs],
        in_specs=[SMEM] + [VMEM] * (len(ins) - 1),
        out_specs=[VMEM] * len(outs),
        name=name,
        compiler_params=pltpu.CompilerParams(vmem_limit_bytes=40 * 2**20),
    )(*ins)


def lanes(block, width=128):
    return pl.ds(pl.multiple_of(block * width, width), width)


def pack_kernel(place, tokens, out_grad, *packs):
    for p, pack in enumerate(packs):
        wanted = jnp.bitwise_xor(place[0], p)
        for m in range(8):
            pack[:, m * 128 : (m + 1) * 128] = tokens[:, lanes(4 * m + wanted)]
        pack[:, 1024:] = out_grad[...]


def weight_grad_kernel(place, p0, p1, p2, p3, out):
    both = jnp.concatenate([p[...] for p in (p0, p1, p2, p3)], axis=0)
    grads = both[:, 1024:]
    for half in range(4):
        cols = slice(half * 256, (half + 1) * 256)
        out[cols, :] = lax.dot_general(
            both[:, cols], grads, (((0,), (0,)), ((), ())), preferred_element_type=F32
        )


def project_kernel(place, p0, p1, p2, p3, own, f1, f2, f3, b1, b2, b3, far_lo, far_hi, *rest):
    values, grads, weight = rest[:4], rest[4:8], rest[8]
    m = place[1]

    def rows(shift, extra=0, size=128):
        return pl.ds(pl.multiple_of(lax.rem(m + 8 + shift, 8) * 128 + extra, 64), size)

    for shift, block in ((0, own), (-1, f1), (-2, f2), (-3, f3), (1, b1), (2, b2), (3, b3)):
        weight[rows(shift), :] = block[...]
    weight[rows(4, 0, 64), :] = far_lo[...]
    weight[rows(4, 64, 64), :] = far_hi[...]
    both = jnp.concatenate([p[...] for p in (p0, p1, p2, p3)], axis=0)
    total = jnp.dot(both[:, :1024], weight[...], preferred_element_type=F32)
    for p in range(4):
        values[p][...] = total[p * 128 : (p + 1) * 128]
    for part in range(4):
        cols = slice(part * 256, (part + 1) * 256)
        piece = lax.dot_general(
            both[:, 1024:], weight[cols, :], (((1,), (1,)), ((), ())), preferred_element_type=F32
        ).astype(BF16)
        for p in range(4):
            grads[p][:, cols] = piece[p * 128 : (p + 1) * 128]


def finish_kernel(place, v0, v1, v2, v3, g0, g1, g2, g3, values, input_grad):
    values[...] = (v0[...] + v1[...] + v2[...] + v3[...]).astype(BF16)
    for p, grad in enumerate((g0, g1, g2, g3)):
        wanted = jnp.bitwise_xor(place[0], p)
        for m in range(8):
            input_grad[:, lanes(4 * m + wanted)] = grad[:, m * 128 : (m + 1) * 128]


def outer_kernel(chosen, outer, momentum, snaps, new_outer, new_momentum):
    k = chosen[0]
    new_outer[...] = outer[...]
    new_momentum[...] = momentum[...]
    now = outer[k]
    pseudo = jnp.zeros_like(now)
    for r in range(16):
        pseudo += now - snaps[r].astype(F32)
    pseudo = pseudo * (1.0 / 16)
    moment = 0.9 * momentum[k] + pseudo
    new_momentum[k] = moment
    new_outer[k] = now - 0.7 * (pseudo + 0.9 * moment)


def partner(core, z):
    return z ^ 1 if core == 0 else ((z + 1) % 16 if z % 2 else (z - 1) % 16)


def swaps():
    z_pairs, diagonal = [], []
    for core in range(2):
        for z in range(16):
            here, there = core * 16 + z, core * 16 + partner(core, z)
            z_pairs.append((here, there))
            diagonal += [(2 * here + y, 2 * there + 1 - y) for y in range(2)]
    return (
        lambda a: a,
        lambda a: lax.ppermute(a, "yhi", [(0, 1), (1, 0)]),
        lambda a: lax.ppermute(a, ("core", "z"), z_pairs),
        lambda a: lax.ppermute(a, ("core", "z", "yhi"), diagonal),
    )


def body(tokens, v_weight, out_grad, outer_params, momentum, snapshot, frag_index):
    z, y = lax.axis_index("z"), lax.axis_index("yhi")
    place = jnp.stack([2 * lax.rem(z, 2) + y, lax.div(z, 2)]).astype(jnp.int32)
    swap = swaps()

    snap = lax.dynamic_index_in_dim(snapshot[0], frag_index[0], 0, keepdims=False)
    snaps = lax.all_gather(snap, REPLICA, axis=0)

    packs = local(pack_kernel, [((128, 1536), BF16)] * 4, "pack", (place, tokens, out_grad))
    packs = [swap[p](packs[p]) for p in range(4)]

    (partial,) = local(weight_grad_kernel, [((1024, 512), F32)], "weight_grad", (place, *packs))
    rings = [[z_of for z_of in range(16) if z_of % 2 == odd] for odd in range(2)]
    summed = lax.psum_scatter(partial, "z", scatter_dimension=0, axis_index_groups=rings, tiled=True)
    weight_grad = (summed * (1.0 / math.sqrt(4096))).astype(BF16)[None]

    own = v_weight[0]
    ahead = functools.partial(lax.ppermute, axis_name="z", perm=[(i, (i + 2) % 16) for i in range(16)])
    behind = functools.partial(lax.ppermute, axis_name="z", perm=[(i, (i - 2) % 16) for i in range(16)])
    fwd, bwd = [own], [own]
    for _ in range(3):
        fwd.append(ahead(fwd[-1]))
        bwd.append(behind(bwd[-1]))
    far = [ahead(fwd[-1][:64]), behind(bwd[-1][64:])]
    parts = pl.pallas_call(
        project_kernel,
        out_shape=[jax.ShapeDtypeStruct((128, 512), F32)] * 4 + [jax.ShapeDtypeStruct((128, 1024), BF16)] * 4,
        in_specs=[SMEM] + [VMEM] * 13,
        out_specs=[VMEM] * 8,
        scratch_shapes=[pltpu.VMEM((1024, 512), BF16)],
        name="project",
        compiler_params=pltpu.CompilerParams(vmem_limit_bytes=40 * 2**20),
    )(place, *packs, own, *fwd[1:], *bwd[1:], *far)
    parts = [swap[i % 4](part) for i, part in enumerate(parts)]
    values, input_grad = local(
        finish_kernel, [((128, 512), BF16), ((128, 4096), BF16)], "finish", (place, *parts)
    )

    new_outer, new_momentum = local(
        outer_kernel,
        [((4, 128, 512), F32)] * 2,
        "outer",
        (frag_index, outer_params, momentum, snaps),
    )
    return (values, input_grad, weight_grad, new_outer, new_momentum)


def solution(mesh):
    fine = Mesh(mesh.devices.reshape(2, 4, 2, 16, 2), EVERY)
    fsdp = ("z", "yhi")
    in_specs = (
        P(EVERY, None),
        P(REPLICA, fsdp, None),
        P(EVERY, None),
        P(None, fsdp, None),
        P(None, fsdp, None),
        P(REPLICA, None, fsdp, None),
        P(),
    )
    out_specs = (
        P(EVERY, None),
        P(EVERY, None),
        P(REPLICA, fsdp, None),
        P(None, fsdp, None),
        P(None, fsdp, None),
    )
    return jax.shard_map(body, mesh=fine, in_specs=in_specs, out_specs=out_specs, check_vma=False)
```

time: 376 us -> 161 us (0.43)
  the two profiles are of different devices: /device:TPU:24 before, /device:TPU:4 now
where the time goes in v1:
time: 161 us; the launch traced here: 160 us
  starting transfers between devices  78.8 us (49%)
  waiting for transfers between devices  48.5 us (30%)
  between operations  16.4 us (10%)
  Pallas kernels  9.07 us (6%)
  local copies, waits for them, and re-layouts  5.93 us (4%)
  other arithmetic  1.7 us (1%)
    ppermute x3, starting transfers between devices, body(): bwd.append(behind(bwd[-1]))  26.1 us
    ppermute x3, starting transfers between devices, swaps(): lax.ppermute(a, 'yhi', [(0, 1), (1, 0)])  22.4 us
    ppermute x3, waiting for transfers between devices, swaps(): lax.ppermute(a, ('core', 'z', 'yhi'), diagonal)  13.4 us
    ppermute x2, waiting for transfers between devices, body(): far = [ahead(fwd[-1][:64]), behind(bwd[-1][64:])]  11.7 us
    ppermute x3, waiting for transfers between devices, body(): bwd.append(behind(bwd[-1]))  11.4 us
    ppermute x2, starting transfers between devices, body(): far = [ahead(fwd[-1][:64]), behind(bwd[-1][64:])]  9.68 us
    ppermute x3, starting transfers between devices, swaps(): lax.ppermute(a, ('core', 'z'), z_pairs)  7.67 us
    ppermute x3, starting transfers between devices, swaps(): lax.ppermute(a, ('core', 'z', 'yhi'), diagonal)  7.2 us
  transfers between devices with their start and end apart: 19, of which 15 were waited for; matrix products, arithmetic and copies ran while one was open for 0% of the time, Pallas kernels for 6%

profile of v1, /device:TPU:4, one launch (start us, length us, event | category | flops | bytes accessed | tf_op | source)
XLA Modules:
  0.0 160.4 jit_solution(12898030050357671665)
XLA Ops:
  12.8 5.1 %collective-permute-start = (bf16[128,1536]{1,0:T(8,128)(2,1)S(1)}, bf16[128,1536]{1,0:T(8,128)(2,1)S(1)}, u32[]{:S(2)}, u32[]{:S(2)}) collective-permute-start(bf16[128,1536]{1,0:T(8,128)(2,1)S(1)} %get-tuple-element.22), channel_id=1, source_target_pairs={{0,1},{1,0},{2,3},{3,2},{4,5},{5,4},{6,7},{7,6},{8,9},{9,8},{10,11... | collective-permute-start | bytes 1179656 | tf_op jit(solution)/shard_map/ppermute | solution.py:111
  18.0 3.8 %collective-permute-start.1 = (bf16[128,1536]{1,0:T(8,128)(2,1)S(1)}, bf16[128,1536]{1,0:T(8,128)(2,1)S(1)}, u32[]{:S(2)}, u32[]{:S(2)}) collective-permute-start(bf16[128,1536]{1,0:T(8,128)(2,1)S(1)} %get-tuple-element.23), channel_id=1, source_target_pairs={{0,2},{2,0},{4,6},{6,4},{8,10},{10,8},{12,14},{14,12},{16,18},{18,... | collective-permute-start | bytes 1179656 | tf_op jit(solution)/shard_map/ppermute | solution.py:112
  21.8 1.9 %collective-permute-start.2 = (bf16[128,1536]{1,0:T(8,128)(2,1)S(1)}, bf16[128,1536]{1,0:T(8,128)(2,1)S(1)}, u32[]{:S(2)}, u32[]{:S(2)}) collective-permute-start(bf16[128,1536]{1,0:T(8,128)(2,1)S(1)} %get-tuple-element.24), channel_id=1, source_target_pairs={{0,3},{1,2},{2,1},{3,0},{4,7},{5,6},{6,5},{7,4},{8,11},{9,10},{10,... | collective-permute-start | bytes 1179656 | tf_op jit(solution)/shard_map/ppermute | solution.py:113
  23.7 3.4 %collective-permute-done.p1 = bf16[128,1536]{1,0:T(8,128)(2,1)S(1)} collective-permute-done((bf16[128,1536]{1,0:T(8,128)(2,1)S(1)}, bf16[128,1536]{1,0:T(8,128)(2,1)S(1)}, u32[]{:S(2)}, u32[]{:S(2)}) %collective-permute-start) | collective-permute-done | bytes 393248 | tf_op jit(solution)/shard_map/ppermute | solution.py:111
  27.6 6.7 %collective-permute-done.2.p3 = bf16[128,1536]{1,0:T(8,128)(2,1)S(1)} collective-permute-done((bf16[128,1536]{1,0:T(8,128)(2,1)S(1)}, bf16[128,1536]{1,0:T(8,128)(2,1)S(1)}, u32[]{:S(2)}, u32[]{:S(2)}) %collective-permute-start.2) | collective-permute-done | bytes 393248 | tf_op jit(solution)/shard_map/ppermute | solution.py:113
  34.3 2.6 %weight_grad.1 = f32[1024,512]{1,0:T(8,128)} custom-call(s32[2]{0:T(128)S(1)} %pad_add_fusion.place, bf16[128,1536]{1,0:T(8,128)(2,1)S(1)} %get-tuple-element.21.p0, bf16[128,1536]{1,0:T(8,128)(2,1)S(1)} %collective-permute-done.p1, bf16[128,1536]{1,0:T(8,128)(2,1)S(1)} %collective-permute-done.1.p2, bf16[128,1536]{1,0:T(8,128)(2,1)S(1)} %collective-permute-done.2.p3), custom_call_target="tpu_custom_call" | custom-call | tf_op jit(solution)/shard_map/weight_grad/pallas_call | solution.py:20
  37.0 13.1 %collective-permute-start.6 = (bf16[128,512]{1,0:T(8,128)(2,1)S(1)}, bf16[128,512]{1,0:T(8,128)(2,1)S(1)}, u32[]{:S(2)}, u32[]{:S(2)}) collective-permute-start(bf16[128,512]{1,0:T(8,128)(2,1)S(1)} %bitcast.11), channel_id=1, source_target_pairs={{0,28},{2,30},{4,0},{6,2},{8,4},{10,6},{12,8},{14,10},{16,12},{18,... | collective-permute-start | bytes 393224 | tf_op jit(solution)/shard_map/ppermute | solution.py:139
  50.0 1.9 %collective-permute-start.3 = (bf16[128,512]{1,0:T(8,128)(2,1)S(1)}, bf16[128,512]{1,0:T(8,128)(2,1)S(1)}, u32[]{:S(2)}, u32[]{:S(2)}) collective-permute-start(bf16[128,512]{1,0:T(8,128)(2,1)S(1)} %bitcast.12), channel_id=1, source_target_pairs={{0,4},{2,6},{4,8},{6,10},{8,12},{10,14},{12,16},{14,18},{16,20},{1... | collective-permute-start | bytes 393224 | tf_op jit(solution)/shard_map/ppermute | solution.py:138
  52.0 2.0 %collective-permute-done.6.b1 = bf16[128,512]{1,0:T(8,128)(2,1)S(1)} collective-permute-done((bf16[128,512]{1,0:T(8,128)(2,1)S(1)}, bf16[128,512]{1,0:T(8,128)(2,1)S(1)}, u32[]{:S(2)}, u32[]{:S(2)}) %collective-permute-start.6) | collective-permute-done | bytes 131104 | tf_op jit(solution)/shard_map/ppermute | solution.py:139
  54.0 6.5 %collective-permute-start.7 = (bf16[128,512]{1,0:T(8,128)(2,1)S(1)}, bf16[128,512]{1,0:T(8,128)(2,1)S(1)}, u32[]{:S(2)}, u32[]{:S(2)}) collective-permute-start(bf16[128,512]{1,0:T(8,128)(2,1)S(1)} %collective-permute-done.6.b1), channel_id=1, source_target_pairs={{0,28},{2,30},{4,0},{6,2},{8,4},{10,6},{12,8},{14,10},{16,12},{18,... | collective-permute-start | bytes 393224 | tf_op jit(solution)/shard_map/ppermute | solution.py:139
  60.6 1.9 %collective-permute-start.4 = (bf16[128,512]{1,0:T(8,128)(2,1)S(1)}, bf16[128,512]{1,0:T(8,128)(2,1)S(1)}, u32[]{:S(2)}, u32[]{:S(2)}) collective-permute-start(bf16[128,512]{1,0:T(8,128)(2,1)S(1)} %collective-permute-done.3.f1), channel_id=1, source_target_pairs={{0,4},{2,6},{4,8},{6,10},{8,12},{10,14},{12,16},{14,18},{16,20},{1... | collective-permute-start | bytes 393224 | tf_op jit(solution)/shard_map/ppermute | solution.py:138
  62.5 3.3 %collective-permute-done.7.b2 = bf16[128,512]{1,0:T(8,128)(2,1)S(1)} collective-permute-done((bf16[128,512]{1,0:T(8,128)(2,1)S(1)}, bf16[128,512]{1,0:T(8,128)(2,1)S(1)}, u32[]{:S(2)}, u32[]{:S(2)}) %collective-permute-start.7) | collective-permute-done | bytes 131104 | tf_op jit(solution)/shard_map/ppermute | solution.py:139
  65.7 6.6 %collective-permute-start.8 = (bf16[128,512]{1,0:T(8,128)(2,1)S(1)}, bf16[128,512]{1,0:T(8,128)(2,1)S(1)}, u32[]{:S(2)}, u32[]{:S(2)}) collective-permute-start(bf16[128,512]{1,0:T(8,128)(2,1)S(1)} %collective-permute-done.7.b2), channel_id=1, source_target_pairs={{0,28},{2,30},{4,0},{6,2},{8,4},{10,6},{12,8},{14,10},{16,12},{18,... | collective-permute-start | bytes 393224 | tf_op jit(solution)/shard_map/ppermute | solution.py:139
  72.3 3.3 %collective-permute-done.4.f2 = bf16[128,512]{1,0:T(8,128)(2,1)S(1)} collective-permute-done((bf16[128,512]{1,0:T(8,128)(2,1)S(1)}, bf16[128,512]{1,0:T(8,128)(2,1)S(1)}, u32[]{:S(2)}, u32[]{:S(2)}) %collective-permute-start.4) | collective-permute-done | bytes 131104 | tf_op jit(solution)/shard_map/ppermute | solution.py:138
  75.6 1.9 %collective-permute-start.5 = (bf16[128,512]{1,0:T(8,128)(2,1)S(1)}, bf16[128,512]{1,0:T(8,128)(2,1)S(1)}, u32[]{:S(2)}, u32[]{:S(2)}) collective-permute-start(bf16[128,512]{1,0:T(8,128)(2,1)S(1)} %collective-permute-done.4.f2), channel_id=1, source_target_pairs={{0,4},{2,6},{4,8},{6,10},{8,12},{10,14},{12,16},{14,18},{16,20},{1... | collective-permute-start | bytes 393224 | tf_op jit(solution)/shard_map/ppermute | solution.py:138
  77.5 6.1 %collective-permute-done.8.b3 = bf16[128,512]{1,0:T(8,128)(2,1)S(1)} collective-permute-done((bf16[128,512]{1,0:T(8,128)(2,1)S(1)}, bf16[128,512]{1,0:T(8,128)(2,1)S(1)}, u32[]{:S(2)}, u32[]{:S(2)}) %collective-permute-start.8) | collective-permute-done | bytes 131104 | tf_op jit(solution)/shard_map/ppermute | solution.py:139
  83.6 7.6 %collective-permute-start.10 = (bf16[64,512]{1,0:T(8,128)(2,1)S(1)}, bf16[64,512]{1,0:T(8,128)(2,1)S(1)}, u32[]{:S(2)}, u32[]{:S(2)}) collective-permute-start(bf16[64,512]{1,0:T(8,128)(2,1)S(1)} %slice.9), channel_id=1, source_target_pairs={{0,28},{2,30},{4,0},{6,2},{8,4},{10,6},{12,8},{14,10},{16,12},{18,... | collective-permute-start | bytes 196616 | tf_op jit(solution)/shard_map/ppermute | solution.py:140
  91.6 2.1 %collective-permute-start.9 = (bf16[64,512]{1,0:T(8,128)(2,1)S(1)}, bf16[64,512]{1,0:T(8,128)(2,1)S(1)}, u32[]{:S(2)}, u32[]{:S(2)}) collective-permute-start(bf16[64,512]{1,0:T(8,128)(2,1)S(1)} %slice.8), channel_id=1, source_target_pairs={{0,4},{2,6},{4,8},{6,10},{8,12},{10,14},{12,16},{14,18},{16,20},{1... | collective-permute-start | bytes 196616 | tf_op jit(solution)/shard_map/ppermute | solution.py:140
  93.6 2.5 %collective-permute-done.10.far_hi = bf16[64,512]{1,0:T(8,128)(2,1)S(1)} collective-permute-done((bf16[64,512]{1,0:T(8,128)(2,1)S(1)}, bf16[64,512]{1,0:T(8,128)(2,1)S(1)}, u32[]{:S(2)}, u32[]{:S(2)}) %collective-permute-start.10) | collective-permute-done | bytes 65568 | tf_op jit(solution)/shard_map/ppermute | solution.py:140
  96.2 9.2 %collective-permute-done.9.far_lo = bf16[64,512]{1,0:T(8,128)(2,1)S(1)} collective-permute-done((bf16[64,512]{1,0:T(8,128)(2,1)S(1)}, bf16[64,512]{1,0:T(8,128)(2,1)S(1)}, u32[]{:S(2)}, u32[]{:S(2)}) %collective-permute-start.9) | collective-permute-done | bytes 65568 | tf_op jit(solution)/shard_map/ppermute | solution.py:140
  105.3 1.9 %project.1 = (f32[128,512]{1,0:T(8,128)S(1)}, f32[128,512]{1,0:T(8,128)S(1)}, f32[128,512]{1,0:T(8,128)S(1)}, f32[128,512]{1,0:T(8,128)S(1)}, bf16[128,1024]{1,0...) custom-call(s32[2]{0:T(128)S(1)} %pad_add_fusion.place, ...), custom_call_target="tpu_custom_call" | custom-call | tf_op jit(solution)/shard_map/project/pallas_call | solution.py:141
  107.2 11.8 %collective-permute-start.11 = (f32[128,512]{1,0:T(8,128)S(1)}, f32[128,512]{1,0:T(8,128)S(1)}, u32[]{:S(2)}, u32[]{:S(2)}) collective-permute-start(f32[128,512]{1,0:T(8,128)S(1)} %get-tuple-element.26), channel_id=1, source_target_pairs={{0,1},{1,0},{2,3},{3,2},{4,5},{5,4},{6,7},{7,6},{8,9},{9,8},{10,11... | collective-permute-start | bytes 786440 | tf_op jit(solution)/shard_map/ppermute | solution.py:111
  119.1 1.9 %collective-permute-start.12 = (f32[128,512]{1,0:T(8,128)S(1)}, f32[128,512]{1,0:T(8,128)S(1)}, u32[]{:S(2)}, u32[]{:S(2)}) collective-permute-start(f32[128,512]{1,0:T(8,128)S(1)} %get-tuple-element.27), channel_id=1, source_target_pairs={{0,2},{2,0},{4,6},{6,4},{8,10},{10,8},{12,14},{14,12},{16,18},{18,... | collective-permute-start | bytes 786440 | tf_op jit(solution)/shard_map/ppermute | solution.py:112
  121.0 3.4 %collective-permute-start.13 = (f32[128,512]{1,0:T(8,128)S(1)}, f32[128,512]{1,0:T(8,128)S(1)}, u32[]{:S(2)}, u32[]{:S(2)}) collective-permute-start(f32[128,512]{1,0:T(8,128)S(1)} %get-tuple-element.28), channel_id=1, source_target_pairs={{0,3},{1,2},{2,1},{3,0},{4,7},{5,6},{6,5},{7,4},{8,11},{9,10},{10,... | collective-permute-start | bytes 786440 | tf_op jit(solution)/shard_map/ppermute | solution.py:113
  124.4 5.4 %collective-permute-start.14 = (bf16[128,1024]{1,0:T(8,128)(2,1)S(1)}, bf16[128,1024]{1,0:T(8,128)(2,1)S(1)}, u32[]{:S(2)}, u32[]{:S(2)}) collective-permute-start(bf16[128,1024]{1,0:T(8,128)(2,1)S(1)} %get-tuple-element.30), channel_id=1, source_target_pairs={{0,1},{1,0},{2,3},{3,2},{4,5},{5,4},{6,7},{7,6},{8,9},{9,8},{10,11... | collective-permute-start | bytes 786440 | tf_op jit(solution)/shard_map/ppermute | solution.py:111
  129.8 1.9 %collective-permute-start.15 = (bf16[128,1024]{1,0:T(8,128)(2,1)S(1)}, bf16[128,1024]{1,0:T(8,128)(2,1)S(1)}, u32[]{:S(2)}, u32[]{:S(2)}) collective-permute-start(bf16[128,1024]{1,0:T(8,128)(2,1)S(1)} %get-tuple-element.31), channel_id=1, source_target_pairs={{0,2},{2,0},{4,6},{6,4},{8,10},{10,8},{12,14},{14,12},{16,18},{18,... | collective-permute-start | bytes 786440 | tf_op jit(solution)/shard_map/ppermute | solution.py:112
  131.7 2.4 %collective-permute-done.11.v1 = f32[128,512]{1,0:T(8,128)S(1)} collective-permute-done((f32[128,512]{1,0:T(8,128)S(1)}, f32[128,512]{1,0:T(8,128)S(1)}, u32[]{:S(2)}, u32[]{:S(2)}) %collective-permute-start.11) | collective-permute-done | bytes 262176 | tf_op jit(solution)/shard_map/ppermute | solution.py:111
  134.1 1.9 %collective-permute-start.16 = (bf16[128,1024]{1,0:T(8,128)(2,1)S(1)}, bf16[128,1024]{1,0:T(8,128)(2,1)S(1)}, u32[]{:S(2)}, u32[]{:S(2)}) collective-permute-start(bf16[128,1024]{1,0:T(8,128)(2,1)S(1)} %get-tuple-element.32), channel_id=1, source_target_pairs={{0,3},{1,2},{2,1},{3,0},{4,7},{5,6},{6,5},{7,4},{8,11},{9,10},{10,... | collective-permute-start | bytes 786440 | tf_op jit(solution)/shard_map/ppermute | solution.py:113
  138.1 6.7 %collective-permute-done.16.g3 = bf16[128,1024]{1,0:T(8,128)(2,1)S(1)} collective-permute-done((bf16[128,1024]{1,0:T(8,128)(2,1)S(1)}, bf16[128,1024]{1,0:T(8,128)(2,1)S(1)}, u32[]{:S(2)}, u32[]{:S(2)}) %collective-permute-start.16) | collective-permute-done | bytes 262176 | tf_op jit(solution)/shard_map/ppermute | solution.py:113
  144.8 1.8 %finish.1 = (bf16[128,512]{1,0:T(8,128)(2,1)}, bf16[128,4096]{1,0:T(8,128)(2,1)}) custom-call(s32[2]{0:T(128)S(1)} %pad_add_fusion.place, f32[128,512]{1,0:T(8,128)S(1)} %get-tuple-element.25.v0, f32[128,512]{1,0:T(8,128)S(1)} %collective-permute-done.11.v1, f32[128,512]{1,0:T(8,128)S(1)} %collective-permute-done.12.v2, ...), custom_call_target="tpu_custom_call" | custom-call | tf_op jit(solution)/shard_map/finish/pallas_call | solution.py:20
  149.5 1.9 %outer.2 = (f32[4,128,512]{2,1,0:T(8,128)}, f32[4,128,512]{2,1,0:T(8,128)}) custom-call(s32[1]{0:T(128)} %copy.13.chosen, f32[4,128,512]{2,1,0:T(8,128)S(1)} %copy-done.2, f32[4,128,512]{2,1,0:T(8,128)S(1)} %copy-done.3, bf16[16,128,512]{2,1,0:T(8,128)(2,1)S(1)} %bitcast.10), custom_call_target="tpu_custom_call" | custom-call | tf_op jit(solution)/shard_map/outer/pallas_call | solution.py:20
  151.4 1.6 %fusion = bf16[1,128,512]{2,1,0:T(8,128)(2,1)} fusion(f32[128,512]{1,0:T(8,128)} %reduce-scatter.2.cloned.1.call-done), kind=kLoop, calls=%fused_computation.1 | loop fusion | flops 131072 | bytes 393216 | tf_op jit(solution)/shard_map/broadcast_in_dim | solution.py:131
  (32 shorter events, 9.9 us)
Async XLA Ops:
  8.0 1.1 copy-start
  8.0 138.6 %all-gather.3.cloned.1.call-start = ((), (), s32[]{:S(2)}) async-start(), calls=%async_computation.2 | async-start | bytes 2228224 | tf_op jit(solution)/shard_map/all_gather | solution.py:123
  9.8 141.6 %reduce-scatter.2.cloned.1.call-start = ((), (), s32[]{:S(2)}) async-start(), calls=%async_computation.1 | async-start | bytes 2359296 | tf_op jit(solution)/shard_map/reduce_scatter | solution.py:130
  9.9 1.2 copy-start.4
  11.1 0.9 copy-start.5
  12.8 14.3 %collective-permute-start = (bf16[128,1536]{1,0:T(8,128)(2,1)S(1)}, bf16[128,1536]{1,0:T(8,128)(2,1)S(1)}, u32[]{:S(2)}, u32[]{:S(2)}) collective-permute-start(bf16[128,1536]{1,0:T(8,128)(2,1)S(1)} %get-tuple-element.22), channel_id=1, source_target_pairs={{0,1},{1,0},{2,3},{3,2},{4,5},{5,4},{6,7},{7,6},{8,9},{9,8},{10,11... | collective-permute-start | bytes 1179656 | tf_op jit(solution)/shard_map/ppermute | solution.py:111
  18.0 9.7 %collective-permute-start.1 = (bf16[128,1536]{1,0:T(8,128)(2,1)S(1)}, bf16[128,1536]{1,0:T(8,128)(2,1)S(1)}, u32[]{:S(2)}, u32[]{:S(2)}) collective-permute-start(bf16[128,1536]{1,0:T(8,128)(2,1)S(1)} %get-tuple-element.23), channel_id=1, source_target_pairs={{0,2},{2,0},{4,6},{6,4},{8,10},{10,8},{12,14},{14,12},{16,18},{18,... | collective-permute-start | bytes 1179656 | tf_op jit(solution)/shard_map/ppermute | solution.py:112
  21.8 12.5 %collective-permute-start.2 = (bf16[128,1536]{1,0:T(8,128)(2,1)S(1)}, bf16[128,1536]{1,0:T(8,128)(2,1)S(1)}, u32[]{:S(2)}, u32[]{:S(2)}) collective-permute-start(bf16[128,1536]{1,0:T(8,128)(2,1)S(1)} %get-tuple-element.24), channel_id=1, source_target_pairs={{0,3},{1,2},{2,1},{3,0},{4,7},{5,6},{6,5},{7,4},{8,11},{9,10},{10,... | collective-permute-start | bytes 1179656 | tf_op jit(solution)/shard_map/ppermute | solution.py:113
  34.3 2.6 %copy-start.6 = (bf16[1,128,512]{2,1,0:T(8,128)(2,1)S(1)}, bf16[1,128,512]{2,1,0:T(8,128)(2,1)}, u32[]{:S(2)}) copy-start(bf16[1,128,512]{2,1,0:T(8,128)(2,1)} %param.8) | copy-start | bytes 393220
  37.0 17.0 %collective-permute-start.6 = (bf16[128,512]{1,0:T(8,128)(2,1)S(1)}, bf16[128,512]{1,0:T(8,128)(2,1)S(1)}, u32[]{:S(2)}, u32[]{:S(2)}) collective-permute-start(bf16[128,512]{1,0:T(8,128)(2,1)S(1)} %bitcast.11), channel_id=1, source_target_pairs={{0,28},{2,30},{4,0},{6,2},{8,4},{10,6},{12,8},{14,10},{16,12},{18,... | collective-permute-start | bytes 393224 | tf_op jit(solution)/shard_map/ppermute | solution.py:139
  50.0 10.5 %collective-permute-start.3 = (bf16[128,512]{1,0:T(8,128)(2,1)S(1)}, bf16[128,512]{1,0:T(8,128)(2,1)S(1)}, u32[]{:S(2)}, u32[]{:S(2)}) collective-permute-start(bf16[128,512]{1,0:T(8,128)(2,1)S(1)} %bitcast.12), channel_id=1, source_target_pairs={{0,4},{2,6},{4,8},{6,10},{8,12},{10,14},{12,16},{14,18},{16,20},{1... | collective-permute-start | bytes 393224 | tf_op jit(solution)/shard_map/ppermute | solution.py:138
  54.0 11.7 %collective-permute-start.7 = (bf16[128,512]{1,0:T(8,128)(2,1)S(1)}, bf16[128,512]{1,0:T(8,128)(2,1)S(1)}, u32[]{:S(2)}, u32[]{:S(2)}) collective-permute-start(bf16[128,512]{1,0:T(8,128)(2,1)S(1)} %collective-permute-done.6.b1), channel_id=1, source_target_pairs={{0,28},{2,30},{4,0},{6,2},{8,4},{10,6},{12,8},{14,10},{16,12},{18,... | collective-permute-start | bytes 393224 | tf_op jit(solution)/shard_map/ppermute | solution.py:139
  60.6 15.0 %collective-permute-start.4 = (bf16[128,512]{1,0:T(8,128)(2,1)S(1)}, bf16[128,512]{1,0:T(8,128)(2,1)S(1)}, u32[]{:S(2)}, u32[]{:S(2)}) collective-permute-start(bf16[128,512]{1,0:T(8,128)(2,1)S(1)} %collective-permute-done.3.f1), channel_id=1, source_target_pairs={{0,4},{2,6},{4,8},{6,10},{8,12},{10,14},{12,16},{14,18},{16,20},{1... | collective-permute-start | bytes 393224 | tf_op jit(solution)/shard_map/ppermute | solution.py:138
  65.7 17.9 %collective-permute-start.8 = (bf16[128,512]{1,0:T(8,128)(2,1)S(1)}, bf16[128,512]{1,0:T(8,128)(2,1)S(1)}, u32[]{:S(2)}, u32[]{:S(2)}) collective-permute-start(bf16[128,512]{1,0:T(8,128)(2,1)S(1)} %collective-permute-done.7.b2), channel_id=1, source_target_pairs={{0,28},{2,30},{4,0},{6,2},{8,4},{10,6},{12,8},{14,10},{16,12},{18,... | collective-permute-start | bytes 393224 | tf_op jit(solution)/shard_map/ppermute | solution.py:139
  75.6 16.0 %collective-permute-start.5 = (bf16[128,512]{1,0:T(8,128)(2,1)S(1)}, bf16[128,512]{1,0:T(8,128)(2,1)S(1)}, u32[]{:S(2)}, u32[]{:S(2)}) collective-permute-start(bf16[128,512]{1,0:T(8,128)(2,1)S(1)} %collective-permute-done.4.f2), channel_id=1, source_target_pairs={{0,4},{2,6},{4,8},{6,10},{8,12},{10,14},{12,16},{14,18},{16,20},{1... | collective-permute-start | bytes 393224 | tf_op jit(solution)/shard_map/ppermute | solution.py:138
  83.6 12.5 %collective-permute-start.10 = (bf16[64,512]{1,0:T(8,128)(2,1)S(1)}, bf16[64,512]{1,0:T(8,128)(2,1)S(1)}, u32[]{:S(2)}, u32[]{:S(2)}) collective-permute-start(bf16[64,512]{1,0:T(8,128)(2,1)S(1)} %slice.9), channel_id=1, source_target_pairs={{0,28},{2,30},{4,0},{6,2},{8,4},{10,6},{12,8},{14,10},{16,12},{18,... | collective-permute-start | bytes 196616 | tf_op jit(solution)/shard_map/ppermute | solution.py:140
  91.6 55.1 %copy-start.2 = (f32[4,128,512]{2,1,0:T(8,128)S(1)}, f32[4,128,512]{2,1,0:T(8,128)}, u32[]{:S(2)}) copy-start(f32[4,128,512]{2,1,0:T(8,128)} %outer.3) | copy-start | bytes 3145732
  91.6 13.8 %collective-permute-start.9 = (bf16[64,512]{1,0:T(8,128)(2,1)S(1)}, bf16[64,512]{1,0:T(8,128)(2,1)S(1)}, u32[]{:S(2)}, u32[]{:S(2)}) collective-permute-start(bf16[64,512]{1,0:T(8,128)(2,1)S(1)} %slice.8), channel_id=1, source_target_pairs={{0,4},{2,6},{4,8},{6,10},{8,12},{10,14},{12,16},{14,18},{16,20},{1... | collective-permute-start | bytes 196616 | tf_op jit(solution)/shard_map/ppermute | solution.py:140
  107.2 26.9 %collective-permute-start.11 = (f32[128,512]{1,0:T(8,128)S(1)}, f32[128,512]{1,0:T(8,128)S(1)}, u32[]{:S(2)}, u32[]{:S(2)}) collective-permute-start(f32[128,512]{1,0:T(8,128)S(1)} %get-tuple-element.26), channel_id=1, source_target_pairs={{0,1},{1,0},{2,3},{3,2},{4,5},{5,4},{6,7},{7,6},{8,9},{9,8},{10,11... | collective-permute-start | bytes 786440 | tf_op jit(solution)/shard_map/ppermute | solution.py:111
  119.1 17.0 %collective-permute-start.12 = (f32[128,512]{1,0:T(8,128)S(1)}, f32[128,512]{1,0:T(8,128)S(1)}, u32[]{:S(2)}, u32[]{:S(2)}) collective-permute-start(f32[128,512]{1,0:T(8,128)S(1)} %get-tuple-element.27), channel_id=1, source_target_pairs={{0,2},{2,0},{4,6},{6,4},{8,10},{10,8},{12,14},{14,12},{16,18},{18,... | collective-permute-start | bytes 786440 | tf_op jit(solution)/shard_map/ppermute | solution.py:112
  121.0 15.1 %collective-permute-start.13 = (f32[128,512]{1,0:T(8,128)S(1)}, f32[128,512]{1,0:T(8,128)S(1)}, u32[]{:S(2)}, u32[]{:S(2)}) collective-permute-start(f32[128,512]{1,0:T(8,128)S(1)} %get-tuple-element.28), channel_id=1, source_target_pairs={{0,3},{1,2},{2,1},{3,0},{4,7},{5,6},{6,5},{7,4},{8,11},{9,10},{10,... | collective-permute-start | bytes 786440 | tf_op jit(solution)/shard_map/ppermute | solution.py:113
  124.4 12.6 %collective-permute-start.14 = (bf16[128,1024]{1,0:T(8,128)(2,1)S(1)}, bf16[128,1024]{1,0:T(8,128)(2,1)S(1)}, u32[]{:S(2)}, u32[]{:S(2)}) collective-permute-start(bf16[128,1024]{1,0:T(8,128)(2,1)S(1)} %get-tuple-element.30), channel_id=1, source_target_pairs={{0,1},{1,0},{2,3},{3,2},{4,5},{5,4},{6,7},{7,6},{8,9},{9,8},{10,11... | collective-permute-start | bytes 786440 | tf_op jit(solution)/shard_map/ppermute | solution.py:111
  129.8 8.3 %collective-permute-start.15 = (bf16[128,1024]{1,0:T(8,128)(2,1)S(1)}, bf16[128,1024]{1,0:T(8,128)(2,1)S(1)}, u32[]{:S(2)}, u32[]{:S(2)}) collective-permute-start(bf16[128,1024]{1,0:T(8,128)(2,1)S(1)} %get-tuple-element.31), channel_id=1, source_target_pairs={{0,2},{2,0},{4,6},{6,4},{8,10},{10,8},{12,14},{14,12},{16,18},{18,... | collective-permute-start | bytes 786440 | tf_op jit(solution)/shard_map/ppermute | solution.py:112
  134.1 10.7 %collective-permute-start.16 = (bf16[128,1024]{1,0:T(8,128)(2,1)S(1)}, bf16[128,1024]{1,0:T(8,128)(2,1)S(1)}, u32[]{:S(2)}, u32[]{:S(2)}) collective-permute-start(bf16[128,1024]{1,0:T(8,128)(2,1)S(1)} %get-tuple-element.32), channel_id=1, source_target_pairs={{0,3},{1,2},{2,1},{3,0},{4,7},{5,6},{6,5},{7,4},{8,11},{9,10},{10,... | collective-permute-start | bytes 786440 | tf_op jit(solution)/shard_map/ppermute | solution.py:113
  146.6 1.6 copy-start.1
  148.2 1.2 copy-start.3
Sparse Core Ops, SparseCore 0:
  11.6 49.1 all-gather.2
Sparse Core Ops, SparseCore 1:
  37.0 84.1 reduce-scatter.1

commit v2 on v1

v2 whole, which is shorter than its diff:
```python
import functools
import math

import jax
import jax.numpy as jnp
from jax import lax
from jax.experimental import pallas as pl
from jax.experimental.pallas import tpu as pltpu
from jax.sharding import Mesh
from jax.sharding import PartitionSpec as P

REPLICA = ("ylo", "x", "core")
EVERY = REPLICA + ("z", "yhi")
F32, BF16 = jnp.float32, jnp.bfloat16
VMEM = pl.BlockSpec(memory_space=pltpu.VMEM)
SMEM = pl.BlockSpec(memory_space=pltpu.SMEM)


def local(kernel, outs, name, ins):
    return pl.pallas_call(
        kernel,
        out_shape=[jax.ShapeDtypeStruct(s, d) for s, d in outs],
        in_specs=[SMEM] + [VMEM] * (len(ins) - 1),
        out_specs=[VMEM] * len(outs),
        name=name,
        compiler_params=pltpu.CompilerParams(vmem_limit_bytes=40 * 2**20),
    )(*ins)


def lanes(block, width=128):
    return pl.ds(pl.multiple_of(block * width, width), width)


def pack_kernel(place, tokens, out_grad, *packs):
    for p, pack in enumerate(packs):
        wanted = jnp.bitwise_xor(place[0], min(p, 3))
        for m in range(8):
            pack[:, m * 128 : (m + 1) * 128] = tokens[:, lanes(4 * m + wanted)]
        if p < 4:
            pack[:, 1024:] = out_grad[...]


def weight_grad_kernel(place, p0, p1, p2, p3, out):
    both = jnp.concatenate([p[...] for p in (p0, p1, p2, p3)], axis=0)
    grads = both[:, 1024:]
    for part in range(4):
        cols = slice(part * 256, (part + 1) * 256)
        out[cols, :] = lax.dot_general(
            both[:, cols], grads, (((0,), (0,)), ((), ())), preferred_element_type=F32
        )


def project_kernel(place, own, own_more, other, other_more, gathered, v_own, v_other, g_own, g_other, weight):
    parity = lax.shift_right_logical(place[0], 1)
    for half in range(2):
        for m in range(8):
            row = pl.multiple_of((2 * m + jnp.bitwise_xor(parity, half)) * 128, 128)
            weight[half * 1024 + m * 128 : half * 1024 + (m + 1) * 128, :] = gathered[pl.ds(row, 128), :]
    rows = jnp.concatenate([own[:, :1024], other[:, :1024]], axis=0)
    rows_more = jnp.concatenate([own_more[:, :1024], other_more[...]], axis=0)
    total = jnp.dot(rows, weight[:1024, :], preferred_element_type=F32)
    total += jnp.dot(rows_more, weight[1024:, :], preferred_element_type=F32)
    v_own[...] = total[:128]
    v_other[...] = total[128:]
    grads = jnp.concatenate([own[:, 1024:], other[:, 1024:]], axis=0)
    for part in range(4):
        cols = slice(part * 512, (part + 1) * 512)
        piece = lax.dot_general(
            grads, weight[cols, :], (((1,), (1,)), ((), ())), preferred_element_type=F32
        ).astype(BF16)
        g_own[:, cols] = piece[:128]
        g_other[:, cols] = piece[128:]


def finish_kernel(place, v_own, v_other, g_own, g_other, values, input_grad):
    values[...] = (v_own[...] + v_other[...]).astype(BF16)
    for p in range(4):
        grad = (g_own, g_other)[p % 2]
        wanted = jnp.bitwise_xor(place[0], p)
        for m in range(8):
            at = (p // 2) * 1024 + m * 128
            input_grad[:, lanes(4 * m + wanted)] = grad[:, at : at + 128]


def outer_kernel(chosen, outer, momentum, summed, new_outer, new_momentum):
    k = chosen[0]
    new_outer[...] = outer[...]
    new_momentum[...] = momentum[...]
    pseudo = summed[...] * (1.0 / 16)
    moment = 0.9 * momentum[k] + pseudo
    new_momentum[k] = moment
    new_outer[k] = outer[k] - 0.7 * (pseudo + 0.9 * moment)


def partner(core, z):
    return z ^ 1 if core == 0 else ((z + 1) % 16 if z % 2 else (z - 1) % 16)


def swaps():
    z_pairs, diagonal = [], []
    for core in range(2):
        for z in range(16):
            here, there = core * 16 + z, core * 16 + partner(core, z)
            z_pairs.append((here, there))
            diagonal += [(2 * here + y, 2 * there + 1 - y) for y in range(2)]
    return (
        lambda a: a,
        lambda a: lax.ppermute(a, "yhi", [(0, 1), (1, 0)]),
        lambda a: lax.ppermute(a, ("core", "z"), z_pairs),
        lambda a: lax.ppermute(a, ("core", "z", "yhi"), diagonal),
    )


def body(tokens, v_weight, out_grad, outer_params, momentum, snapshot, frag_index):
    z, y = lax.axis_index("z"), lax.axis_index("yhi")
    place = jnp.stack([2 * lax.rem(z, 2) + y, lax.div(z, 2)]).astype(jnp.int32)
    swap = swaps()
    gathered = lax.all_gather(v_weight[0], "z", axis=0, tiled=True)

    packed = local(pack_kernel, [((128, 1536), BF16)] * 4 + [((128, 1024), BF16)], "pack", (place, tokens, out_grad))
    packs = [swap[p](packed[p]) for p in range(4)]
    (partial,) = local(weight_grad_kernel, [((1024, 512), F32)], "weight_grad", (place, *packs))
    rings = [[z_of for z_of in range(16) if z_of % 2 == odd] for odd in range(2)]
    summed = lax.psum_scatter(partial, "z", scatter_dimension=0, axis_index_groups=rings, tiled=True)
    weight_grad = (summed * (1.0 / math.sqrt(4096))).astype(BF16)[None]

    more, chosen = lax.optimization_barrier((packed[4], frag_index, partial))[:2]
    more = swap[1](more)
    outer_now = lax.dynamic_index_in_dim(outer_params, chosen[0], 0, keepdims=False)
    snap = lax.dynamic_index_in_dim(snapshot[0], chosen[0], 0, keepdims=False)
    exchange = functools.partial(lax.all_to_all, axis_name=REPLICA, split_axis=0, concat_axis=0, tiled=True)
    diff = exchange(outer_now - snap.astype(F32)).reshape(16, 8, 512).sum(0)
    diff = exchange(jnp.tile(diff, (16, 1)))
    new_outer, new_momentum = local(
        outer_kernel, [((4, 128, 512), F32)] * 2, "outer", (chosen, outer_params, momentum, diff)
    )

    place = lax.optimization_barrier((place, new_momentum))[0]
    v_own, v_other, g_own, g_other = pl.pallas_call(
        project_kernel,
        out_shape=[jax.ShapeDtypeStruct((128, 512), F32)] * 2 + [jax.ShapeDtypeStruct((128, 2048), BF16)] * 2,
        in_specs=[SMEM] + [VMEM] * 5,
        out_specs=[VMEM] * 4,
        scratch_shapes=[pltpu.VMEM((2048, 512), BF16)],
        name="project",
        compiler_params=pltpu.CompilerParams(vmem_limit_bytes=40 * 2**20),
    )(place, packs[0], packed[2], packs[1], more, gathered)
    v_own = lax.optimization_barrier((v_own, weight_grad))[0]
    values, input_grad = local(
        finish_kernel,
        [((128, 512), BF16), ((128, 4096), BF16)],
        "finish",
        (place, v_own, swap[1](v_other), g_own, swap[1](g_other)),
    )
    return (values, input_grad, weight_grad, new_outer, new_momentum)


def solution(mesh):
    fine = Mesh(mesh.devices.reshape(2, 4, 2, 16, 2), EVERY)
    fsdp = ("z", "yhi")
    in_specs = (
        P(EVERY, None),
        P(REPLICA, fsdp, None),
        P(EVERY, None),
        P(None, fsdp, None),
        P(None, fsdp, None),
        P(REPLICA, None, fsdp, None),
        P(),
    )
    out_specs = (
        P(EVERY, None),
        P(EVERY, None),
        P(REPLICA, fsdp, None),
        P(None, fsdp, None),
        P(None, fsdp, None),
    )
    return jax.shard_map(body, mesh=fine, in_specs=in_specs, out_specs=out_specs, check_vma=False)
```

time: 161 us -> 140 us (0.87)
  the two profiles are of different devices: /device:TPU:4 before, /device:TPU:24 now
where the time goes in v2:
time: 140 us; the launch traced here: 139 us
  waiting for transfers between devices  61.7 us (44%)
  starting transfers between devices  31.9 us (23%)
  between operations  16.3 us (12%)
  blocking collectives  10.4 us (7%)
  Pallas kernels  8.63 us (6%)
  local copies, waits for them, and re-layouts  5.16 us (4%)
  other arithmetic  4.92 us (4%)
    all_gather x1, waiting for transfers between devices, body(): gathered = lax.all_gather(v_weight[0], 'z', axis=0, tiled=True)  39.6 us
    ppermute x4, waiting for transfers between devices, swaps(): lax.ppermute(a, 'yhi', [(0, 1), (1, 0)])  18.3 us
    ppermute x4, starting transfers between devices, swaps(): lax.ppermute(a, 'yhi', [(0, 1), (1, 0)])  14 us
    all_to_all x1, blocking collectives, body(): diff = exchange(jnp.tile(diff, (16, 1)))  10.4 us
    all_to_all x1, starting transfers between devices, body(): diff = exchange(outer_now - snap.astype(F32)).reshape(16, 8, 512).sum(0)  10.3 us
    pallas_call x4, Pallas kernels, local(): pl.pallas_call(kernel, out_shape=[jax.ShapeDtypeStruct(s, d) for s, d in...  6.84 us
    ppermute x1, starting transfers between devices, swaps(): lax.ppermute(a, ('core', 'z', 'yhi'), diagonal)  5.56 us
    unnamed x12, local copies, waits for them, and re-layouts  4.42 us
  transfers between devices with their start and end apart: 9, of which 4 were waited for; matrix products, arithmetic and copies ran while one was open for 4% of the time, Pallas kernels for 5%

profile of v2, /device:TPU:24, one launch (start us, length us, event | category | flops | bytes accessed | tf_op | source)
XLA Modules:
  0.0 139.1 jit_solution(2952801539692755762)
XLA Ops:
  8.0 0.0 all-gather.3.cloned.1.call-start
  8.0 0.7 all-gather.3.cloned.1.call-update
  8.7 0.0 reduce-scatter.2.cloned.1.call-start
  8.8 0.1 pad_add_fusion.place
  8.9 1.2 copy-done.3
  10.1 0.9 copy-done.4
  11.0 0.9 pack.1
  11.9 0.0 copy-start.5
  11.9 0.7 copy-done.5
  12.6 3.1 %collective-permute-start = (bf16[128,1536]{1,0:T(8,128)(2,1)S(1)}, bf16[128,1536]{1,0:T(8,128)(2,1)S(1)}, u32[]{:S(2)}, u32[]{:S(2)}) collective-permute-start(bf16[128,1536]{1,0:T(8,128)(2,1)S(1)} %get-tuple-element.24), channel_id=1, source_target_pairs={{0,1},{1,0},{2,3},{3,2},{4,5},{5,4},{6,7},{7,6},{8,9},{9,8},{10,11... | collective-permute-start | bytes 1179656 | tf_op jit(solution)/shard_map/ppermute | solution.py:108
  15.7 5.6 %collective-permute-start.2 = (bf16[128,1536]{1,0:T(8,128)(2,1)S(1)}, bf16[128,1536]{1,0:T(8,128)(2,1)S(1)}, u32[]{:S(2)}, u32[]{:S(2)}) collective-permute-start(bf16[128,1536]{1,0:T(8,128)(2,1)S(1)} %get-tuple-element.26), channel_id=1, source_target_pairs={{0,3},{1,2},{2,1},{3,0},{4,7},{5,6},{6,5},{7,4},{8,11},{9,10},{10,... | collective-permute-start | bytes 1179656 | tf_op jit(solution)/shard_map/ppermute | solution.py:110
  21.3 2.0 %collective-permute-start.1 = (bf16[128,1536]{1,0:T(8,128)(2,1)S(1)}, bf16[128,1536]{1,0:T(8,128)(2,1)S(1)}, u32[]{:S(2)}, u32[]{:S(2)}) collective-permute-start(bf16[128,1536]{1,0:T(8,128)(2,1)S(1)} %get-tuple-element.25.own_more), channel_id=1, source_target_pairs={{0,2},{2,0},{4,6},{6,4},{8,10},{10,8},{12,14},{14,12},{16,18},{18,... | collective-permute-start | bytes 1179656 | tf_op jit(solution)/shard_map/ppermute | solution.py:109
  23.3 11.9 %collective-permute-done.p1.other = bf16[128,1536]{1,0:T(8,128)(2,1)S(1)} collective-permute-done((bf16[128,1536]{1,0:T(8,128)(2,1)S(1)}, bf16[128,1536]{1,0:T(8,128)(2,1)S(1)}, u32[]{:S(2)}, u32[]{:S(2)}) %collective-permute-start) | collective-permute-done | bytes 393248 | tf_op jit(solution)/shard_map/ppermute | solution.py:108
  35.3 2.6 %weight_grad.1 = f32[1024,512]{1,0:T(8,128)} custom-call(s32[2]{0:T(128)S(1)} %pad_add_fusion.place, bf16[128,1536]{1,0:T(8,128)(2,1)S(1)} %get-tuple-element.23.p0.own, bf16[128,1536]{1,0:T(8,128)(2,1)S(1)} %collective-permute-done.p1.other, bf16[128,1536]{1,0:T(8,128)(2,1)S(1)} %collective-permute-done.1.p2, bf16[128,1536]{1,0:T(8,128)(2,1)S(1)} %collective-permute-done.2.p3), custom_call_target="tpu_custom_call" | custom-call | tf_op jit(solution)/shard_map/weight_grad/pallas_call | solution.py:20
  37.9 0.0 reduce-scatter.2.cloned.1.call-update
  38.7 1.6 %convert_subtract_fusion = f32[16,8,512]{2,1,0:T(8,128)} fusion(f32[4,128,512]{2,1,0:T(8,128)S(1)} %copy-done.1, s32[]{:T(128)S(6)} %select_n.6, bf16[1,4,128,512]{3,2,1,0:T(8,128)(2,1)} %param.12), kind=kLoop, calls=%fused_computation | loop fusion | flops 131072 | bytes 655364 | tf_op jit(solution)/shard_map/sub | solution.py:132
  40.3 10.3 %all-to-all-start = ((f32[16,8,512]{2,1,0:T(8,128)}), f32[16,8,512]{2,1,0:T(8,128)}, u32[]{:S(2)}, u32[]{:S(2)}) async-start(f32[16,8,512]{2,1,0:T(8,128)} %convert_subtract_fusion), calls=%async_computation | async-start | bytes 524288 | tf_op jit(solution)/shard_map/all_to_all | solution.py:132
  50.6 3.5 %collective-permute-start.3 = (bf16[128,1024]{1,0:T(8,128)(2,1)}, bf16[128,1024]{1,0:T(8,128)(2,1)S(1)}, u32[]{:S(2)}, u32[]{:S(2)}) collective-permute-start(bf16[128,1024]{1,0:T(8,128)(2,1)} %copy-done.5), channel_id=1, source_target_pairs={{0,1},{1,0},{2,3},{3,2},{4,5},{5,4},{6,7},{7,6},{8,9},{9,8},{10,11... | collective-permute-start | bytes 786440 | tf_op jit(solution)/shard_map/ppermute | solution.py:108
  54.1 3.1 %all-to-all-done = f32[16,8,512]{2,1,0:T(8,128)} async-done(((f32[16,8,512]{2,1,0:T(8,128)}), f32[16,8,512]{2,1,0:T(8,128)}, u32[]{:S(2)}, u32[]{:S(2)}) %all-to-all-start) | async-done | bytes 262176 | tf_op jit(solution)/shard_map/all_to_all | solution.py:132
  57.2 1.6 %reduce_sum.9 = f32[8,512]{1,0:T(8,128)} reduce(f32[16,8,512]{2,1,0:T(8,128)} %all-to-all-done, f32[]{:T(128)} %constant.28.clone.1), dimensions={0}, to_apply=%region_0.0 | reduce | flops 61440 | bytes 278532 | tf_op jit(solution)/shard_map/reduce_sum | solution.py:132
  58.8 0.7 tile.2
  59.5 10.4 %all_to_all.14 = f32[16,8,512]{2,1,0:T(8,128)S(1)} all-to-all(f32[16,8,512]{2,1,0:T(8,128)S(1)} %tile.2), channel_id=1, replica_groups=mesh['ylo'=2,'x'=4,'core'=2,'z'=16,'yhi'=2] {'ylo','x','core'}, dimensions={0} | all-to-all | bytes 524288 | tf_op jit(solution)/shard_map/all_to_all | solution.py:133
  69.9 1.5 %outer.2 = (f32[4,128,512]{2,1,0:T(8,128)}, f32[4,128,512]{2,1,0:T(8,128)}) custom-call(s32[1]{0:T(128)} %copy.12.chosen, f32[4,128,512]{2,1,0:T(8,128)S(1)} %copy-done.1, f32[4,128,512]{2,1,0:T(8,128)S(1)} %copy-done.2, f32[128,512]{1,0:T(8,128)S(1)} %bitcast.16), custom_call_target="tpu_custom_call" | custom-call | tf_op jit(solution)/shard_map/outer/pallas_call | solution.py:20
  71.5 39.6 %all-gather.3.cloned.1.call-done = bf16[1,2048,512]{2,1,0:T(8,128)(2,1)} async-done(((bf16[1,128,512]{2,1,0:T(8,128)(2,1)}), bf16[1,2048,512]{2,1,0:T(8,128)(2,1)}) %all-gather.3.cloned.1.call-update) | async-done | bytes 2097168 | tf_op jit(solution)/shard_map/all_gather | solution.py:118
  111.0 1.6 %copy-done = bf16[1,2048,512]{2,1,0:T(8,128)(2,1)S(1)} copy-done((bf16[1,2048,512]{2,1,0:T(8,128)(2,1)S(1)}, bf16[1,2048,512]{2,1,0:T(8,128)(2,1)}, u32[]{:S(2)}) %copy-start) | copy-done | bytes 2097176
  112.6 1.8 %project.1 = (f32[128,512]{1,0:T(8,128)S(1)}, f32[128,512]{1,0:T(8,128)S(1)}, bf16[128,2048]{1,0:T(8,128)(2,1)S(1)}, bf16[128,2048]{1,0:T(8,128)(2,1)S(1)}) custom-call(s32[2]{0:T(128)S(1)} %pad_add_fusion.place, bf16[128,1536]{1,0:T(8,128)(2,1)S(1)} %get-tuple-element.23.p0.own, bf16[128,1536]{1,0:T(8,128)(2,1)S(1)} %get-tuple-element.25.own_more, ...), custom_call_target="tpu_custom_call" | custom-call | tf_op jit(solution)/shard_map/project/pallas_call | solution.py:139
  114.4 1.9 %collective-permute-start.5 = (bf16[128,2048]{1,0:T(8,128)(2,1)S(1)}, bf16[128,2048]{1,0:T(8,128)(2,1)S(1)}, u32[]{:S(2)}, u32[]{:S(2)}) collective-permute-start(bf16[128,2048]{1,0:T(8,128)(2,1)S(1)} %get-tuple-element.35), channel_id=1, source_target_pairs={{0,1},{1,0},{2,3},{3,2},{4,5},{5,4},{6,7},{7,6},{8,9},{9,8},{10,11... | collective-permute-start | bytes 1572872 | tf_op jit(solution)/shard_map/ppermute | solution.py:108
  116.3 5.4 %collective-permute-start.4 = (f32[128,512]{1,0:T(8,128)S(1)}, f32[128,512]{1,0:T(8,128)S(1)}, u32[]{:S(2)}, u32[]{:S(2)}) collective-permute-start(f32[128,512]{1,0:T(8,128)S(1)} %get-tuple-element.33), channel_id=1, source_target_pairs={{0,1},{1,0},{2,3},{3,2},{4,5},{5,4},{6,7},{7,6},{8,9},{9,8},{10,11... | collective-permute-start | bytes 786440 | tf_op jit(solution)/shard_map/ppermute | solution.py:108
  121.8 0.0 reduce-scatter.2.cloned.1.call-done
  121.8 1.6 %fusion = bf16[1,128,512]{2,1,0:T(8,128)(2,1)} fusion(f32[128,512]{1,0:T(8,128)} %reduce-scatter.2.cloned.1.call-done), kind=kLoop, calls=%fused_computation.2 | loop fusion | flops 131072 | bytes 393216 | tf_op jit(solution)/shard_map/broadcast_in_dim | solution.py:125
  123.4 6.4 %collective-permute-done.4.v_other = f32[128,512]{1,0:T(8,128)S(1)} collective-permute-done((f32[128,512]{1,0:T(8,128)S(1)}, f32[128,512]{1,0:T(8,128)S(1)}, u32[]{:S(2)}, u32[]{:S(2)}) %collective-permute-start.4) | collective-permute-done | bytes 262176 | tf_op jit(solution)/shard_map/ppermute | solution.py:108
  129.8 1.8 %finish.1 = (bf16[128,512]{1,0:T(8,128)(2,1)}, bf16[128,4096]{1,0:T(8,128)(2,1)}) custom-call(s32[2]{0:T(128)S(1)} %pad_add_fusion.place, f32[128,512]{1,0:T(8,128)S(1)} %get-tuple-element.32.v_own, f32[128,512]{1,0:T(8,128)S(1)} %collective-permute-done.4.v_other, bf16[128,2048]{1,0:T(8,128)(2,1)S(1)} %get-tuple-element.34.g_own, ...), custom_call_target="tpu_custom_call" | custom-call | tf_op jit(solution)/shard_map/finish/pallas_call | solution.py:20
  (11 shorter events, 0.0 us)
Async XLA Ops:
  8.0 103.0 %all-gather.3.cloned.1.call-start = ((), (), s32[]{:S(2)}) async-start(), calls=%async_computation.4 | async-start | bytes 2228224 | tf_op jit(solution)/shard_map/all_gather | solution.py:118
  8.7 113.1 %reduce-scatter.2.cloned.1.call-start = ((), (), s32[]{:S(2)}) async-start(), calls=%async_computation.3 | async-start | bytes 2359296 | tf_op jit(solution)/shard_map/reduce_scatter | solution.py:124
  8.9 1.2 copy-start.3
  10.1 0.9 copy-start.4
  11.9 0.7 copy-start.5
  12.6 22.7 %collective-permute-start = (bf16[128,1536]{1,0:T(8,128)(2,1)S(1)}, bf16[128,1536]{1,0:T(8,128)(2,1)S(1)}, u32[]{:S(2)}, u32[]{:S(2)}) collective-permute-start(bf16[128,1536]{1,0:T(8,128)(2,1)S(1)} %get-tuple-element.24), channel_id=1, source_target_pairs={{0,1},{1,0},{2,3},{3,2},{4,5},{5,4},{6,7},{7,6},{8,9},{9,8},{10,11... | collective-permute-start | bytes 1179656 | tf_op jit(solution)/shard_map/ppermute | solution.py:108
  15.7 19.5 %collective-permute-start.2 = (bf16[128,1536]{1,0:T(8,128)(2,1)S(1)}, bf16[128,1536]{1,0:T(8,128)(2,1)S(1)}, u32[]{:S(2)}, u32[]{:S(2)}) collective-permute-start(bf16[128,1536]{1,0:T(8,128)(2,1)S(1)} %get-tuple-element.26), channel_id=1, source_target_pairs={{0,3},{1,2},{2,1},{3,0},{4,7},{5,6},{6,5},{7,4},{8,11},{9,10},{10,... | collective-permute-start | bytes 1179656 | tf_op jit(solution)/shard_map/ppermute | solution.py:110
  21.3 14.0 %collective-permute-start.1 = (bf16[128,1536]{1,0:T(8,128)(2,1)S(1)}, bf16[128,1536]{1,0:T(8,128)(2,1)S(1)}, u32[]{:S(2)}, u32[]{:S(2)}) collective-permute-start(bf16[128,1536]{1,0:T(8,128)(2,1)S(1)} %get-tuple-element.25.own_more), channel_id=1, source_target_pairs={{0,2},{2,0},{4,6},{6,4},{8,10},{10,8},{12,14},{14,12},{16,18},{18,... | collective-permute-start | bytes 1179656 | tf_op jit(solution)/shard_map/ppermute | solution.py:109
  35.3 3.4 %copy-start.1 = (f32[4,128,512]{2,1,0:T(8,128)S(1)}, f32[4,128,512]{2,1,0:T(8,128)}, u32[]{:S(2)}) copy-start(f32[4,128,512]{2,1,0:T(8,128)} %outer.3) | copy-start | bytes 3145732
  37.9 32.0 %copy-start.2 = (f32[4,128,512]{2,1,0:T(8,128)S(1)}, f32[4,128,512]{2,1,0:T(8,128)}, u32[]{:S(2)}) copy-start(f32[4,128,512]{2,1,0:T(8,128)} %momentum.1) | copy-start | bytes 3145732
  40.3 16.9 %all-to-all-start = ((f32[16,8,512]{2,1,0:T(8,128)}), f32[16,8,512]{2,1,0:T(8,128)}, u32[]{:S(2)}, u32[]{:S(2)}) async-start(f32[16,8,512]{2,1,0:T(8,128)} %convert_subtract_fusion), calls=%async_computation | async-start | bytes 524288 | tf_op jit(solution)/shard_map/all_to_all | solution.py:132
  50.6 20.9 %collective-permute-start.3 = (bf16[128,1024]{1,0:T(8,128)(2,1)}, bf16[128,1024]{1,0:T(8,128)(2,1)S(1)}, u32[]{:S(2)}, u32[]{:S(2)}) collective-permute-start(bf16[128,1024]{1,0:T(8,128)(2,1)} %copy-done.5), channel_id=1, source_target_pairs={{0,1},{1,0},{2,3},{3,2},{4,5},{5,4},{6,7},{7,6},{8,9},{9,8},{10,11... | collective-permute-start | bytes 786440 | tf_op jit(solution)/shard_map/ppermute | solution.py:108
  111.0 1.6 %copy-start = (bf16[1,2048,512]{2,1,0:T(8,128)(2,1)S(1)}, bf16[1,2048,512]{2,1,0:T(8,128)(2,1)}, u32[]{:S(2)}) copy-start(bf16[1,2048,512]{2,1,0:T(8,128)(2,1)} %all-gather.3.cloned.1.call-done) | copy-start | bytes 6291460
  114.4 15.4 %collective-permute-start.5 = (bf16[128,2048]{1,0:T(8,128)(2,1)S(1)}, bf16[128,2048]{1,0:T(8,128)(2,1)S(1)}, u32[]{:S(2)}, u32[]{:S(2)}) collective-permute-start(bf16[128,2048]{1,0:T(8,128)(2,1)S(1)} %get-tuple-element.35), channel_id=1, source_target_pairs={{0,1},{1,0},{2,3},{3,2},{4,5},{5,4},{6,7},{7,6},{8,9},{9,8},{10,11... | collective-permute-start | bytes 1572872 | tf_op jit(solution)/shard_map/ppermute | solution.py:108
  116.3 13.5 %collective-permute-start.4 = (f32[128,512]{1,0:T(8,128)S(1)}, f32[128,512]{1,0:T(8,128)S(1)}, u32[]{:S(2)}, u32[]{:S(2)}) collective-permute-start(f32[128,512]{1,0:T(8,128)S(1)} %get-tuple-element.33), channel_id=1, source_target_pairs={{0,1},{1,0},{2,3},{3,2},{4,5},{5,4},{6,7},{7,6},{8,9},{9,8},{10,11... | collective-permute-start | bytes 786440 | tf_op jit(solution)/shard_map/ppermute | solution.py:108
Sparse Core Ops, SparseCore 0:
  10.9 100.0 all-gather.2
Sparse Core Ops, SparseCore 1:
  38.0 78.5 reduce-scatter.1

commit v3 on v2

--- a/solution.py
+++ b/solution.py
@@ -16,12 +16,13 @@
 SMEM = pl.BlockSpec(memory_space=pltpu.SMEM)
 
 
-def local(kernel, outs, name, ins):
+def local(kernel, outs, name, ins, scratch=()):
     return pl.pallas_call(
         kernel,
         out_shape=[jax.ShapeDtypeStruct(s, d) for s, d in outs],
         in_specs=[SMEM] + [VMEM] * (len(ins) - 1),
         out_specs=[VMEM] * len(outs),
+        scratch_shapes=scratch,
         name=name,
         compiler_params=pltpu.CompilerParams(vmem_limit_bytes=40 * 2**20),
     )(*ins)
@@ -50,18 +51,16 @@
         )
 
 
-def project_kernel(place, own, own_more, other, other_more, gathered, v_own, v_other, g_own, g_other, weight):
+def by_class(place, gathered, weight):
     parity = lax.shift_right_logical(place[0], 1)
     for half in range(2):
         for m in range(8):
             row = pl.multiple_of((2 * m + jnp.bitwise_xor(parity, half)) * 128, 128)
             weight[half * 1024 + m * 128 : half * 1024 + (m + 1) * 128, :] = gathered[pl.ds(row, 128), :]
-    rows = jnp.concatenate([own[:, :1024], other[:, :1024]], axis=0)
-    rows_more = jnp.concatenate([own_more[:, :1024], other_more[...]], axis=0)
-    total = jnp.dot(rows, weight[:1024, :], preferred_element_type=F32)
-    total += jnp.dot(rows_more, weight[1024:, :], preferred_element_type=F32)
-    v_own[...] = total[:128]
-    v_other[...] = total[128:]
+
+
+def input_grad_kernel(place, own, other, gathered, g_own, g_other, weight):
+    by_class(place, gathered, weight)
     grads = jnp.concatenate([own[:, 1024:], other[:, 1024:]], axis=0)
     for part in range(4):
         cols = slice(part * 512, (part + 1) * 512)
@@ -70,6 +69,16 @@
         ).astype(BF16)
         g_own[:, cols] = piece[:128]
         g_other[:, cols] = piece[128:]
+
+
+def values_kernel(place, own, own_more, other, other_more, gathered, v_own, v_other, weight):
+    by_class(place, gathered, weight)
+    rows = jnp.concatenate([own[:, :1024], other[:, :1024]], axis=0)
+    rows_more = jnp.concatenate([own_more[:, :1024], other_more[...]], axis=0)
+    total = jnp.dot(rows, weight[:1024, :], preferred_element_type=F32)
+    total += jnp.dot(rows_more, weight[1024:, :], preferred_element_type=F32)
+    v_own[...] = total[:128]
+    v_other[...] = total[128:]
 
 
 def finish_kernel(place, v_own, v_other, g_own, g_other, values, input_grad):
@@ -119,32 +128,37 @@
 
     packed = local(pack_kernel, [((128, 1536), BF16)] * 4 + [((128, 1024), BF16)], "pack", (place, tokens, out_grad))
     packs = [swap[p](packed[p]) for p in range(4)]
-    (partial,) = local(weight_grad_kernel, [((1024, 512), F32)], "weight_grad", (place, *packs))
+    exchange = functools.partial(lax.all_to_all, axis_name=REPLICA, split_axis=0, concat_axis=0, tiled=True)
+    outer_now = lax.dynamic_index_in_dim(outer_params, frag_index[0], 0, keepdims=False)
+    snap = lax.dynamic_index_in_dim(snapshot[0], frag_index[0], 0, keepdims=False)
+    ready, *_ = lax.optimization_barrier((outer_now - snap.astype(F32), packed[0]))
+    diffs = exchange(ready)
+
+    mine = lax.optimization_barrier((packs[0], diffs))[0]
+    (partial,) = local(weight_grad_kernel, [((1024, 512), F32)], "weight_grad", (place, mine, *packs[1:]))
     rings = [[z_of for z_of in range(16) if z_of % 2 == odd] for odd in range(2)]
     summed = lax.psum_scatter(partial, "z", scatter_dimension=0, axis_index_groups=rings, tiled=True)
     weight_grad = (summed * (1.0 / math.sqrt(4096))).astype(BF16)[None]
 
-    more, chosen = lax.optimization_barrier((packed[4], frag_index, partial))[:2]
+    more, diffs = lax.optimization_barrier((packed[4], diffs, partial))[:2]
     more = swap[1](more)
-    outer_now = lax.dynamic_index_in_dim(outer_params, chosen[0], 0, keepdims=False)
-    snap = lax.dynamic_index_in_dim(snapshot[0], chosen[0], 0, keepdims=False)
-    exchange = functools.partial(lax.all_to_all, axis_name=REPLICA, split_axis=0, concat_axis=0, tiled=True)
-    diff = exchange(outer_now - snap.astype(F32)).reshape(16, 8, 512).sum(0)
-    diff = exchange(jnp.tile(diff, (16, 1)))
+    diff = exchange(jnp.tile(diffs.reshape(16, 8, 512).sum(0), (16, 1)))
     new_outer, new_momentum = local(
-        outer_kernel, [((4, 128, 512), F32)] * 2, "outer", (chosen, outer_params, momentum, diff)
+        outer_kernel, [((4, 128, 512), F32)] * 2, "outer", (frag_index, outer_params, momentum, diff)
     )
 
     place = lax.optimization_barrier((place, new_momentum))[0]
-    v_own, v_other, g_own, g_other = pl.pallas_call(
-        project_kernel,
-        out_shape=[jax.ShapeDtypeStruct((128, 512), F32)] * 2 + [jax.ShapeDtypeStruct((128, 2048), BF16)] * 2,
-        in_specs=[SMEM] + [VMEM] * 5,
-        out_specs=[VMEM] * 4,
-        scratch_shapes=[pltpu.VMEM((2048, 512), BF16)],
-        name="project",
-        compiler_params=pltpu.CompilerParams(vmem_limit_bytes=40 * 2**20),
-    )(place, packs[0], packed[2], packs[1], more, gathered)
+    scratch = [pltpu.VMEM((2048, 512), BF16)]
+    g_own, g_other = local(
+        input_grad_kernel, [((128, 2048), BF16)] * 2, "input_grad", (place, packs[0], packs[1], gathered), scratch
+    )
+    v_own, v_other = local(
+        values_kernel,
+        [((128, 512), F32)] * 2,
+        "project",
+        (place, packs[0], packed[2], packs[1], more, gathered),
+        scratch,
+    )
     v_own = lax.optimization_barrier((v_own, weight_grad))[0]
     values, input_grad = local(
         finish_kernel,

time: 140 us -> 139 us (level); the launches traced: 139 us -> 137 us
  blocking collectives: 10.4 us -> 18.4 us
  starting transfers between devices: 31.9 us -> 26.1 us
  waiting for transfers between devices: 61.7 us -> 58 us
  other arithmetic: 4.92 us -> 2.74 us
    ppermute x4, waiting for transfers between devices: 18.3 us -> 4.68 us  [swaps(): lax.ppermute(a, 'yhi', [(0, 1), (1, 0)])]
    all_gather x1, waiting for transfers between devices: 39.6 us -> 49.3 us  [body(): gathered = lax.all_gather(v_weight[0], 'z', axis=0, tiled=True)]
    all_to_all x1, blocking collectives: 10.4 us -> 18.4 us  [body(): diffs = exchange(ready)]
    all_to_all x1, starting transfers between devices: 10.3 us -> 4.84 us  [body(): diff = exchange(jnp.tile(diffs.reshape(16, 8, 512).sum(0), (16, 1)))]
    pallas_call x4 -> x6, Pallas kernels: 6.84 us -> 9.81 us  [local(): pl.pallas_call(kernel, out_shape=[jax.ShapeDtypeStruct(s, d) for s, d in...]
    pallas_call x1 -> x0, Pallas kernels: 1.79 us -> none  [body(): pl.pallas_call(project_kernel, out_shape=[jax.ShapeDtypeStruct((128, 512)...]
    reduce_sum x1, other arithmetic: 1.58 us -> 0.02 us  [body(): diff = exchange(jnp.tile(diffs.reshape(16, 8, 512).sum(0), (16, 1)))]
    unnamed x12 -> x14, local copies, waits for them, and re-layouts: 4.42 us -> 4.43 us
  transfers between devices with their start and end apart: 9 -> 9, of which waited for: 4 -> 3; matrix products, arithmetic and copies ran while one was open for 4% -> 3% of each run, Pallas kernels for 5% -> 6%
where the time goes in v3:
time: 139 us; the launch traced here: 137 us
  waiting for transfers between devices  58 us (42%)
  starting transfers between devices  26.1 us (19%)
  blocking collectives  18.4 us (13%)
  between operations  16.3 us (12%)
  Pallas kernels  9.81 us (7%)
  local copies, waits for them, and re-layouts  5.16 us (4%)
  other arithmetic  2.74 us (2%)
    all_gather x1, waiting for transfers between devices, body(): gathered = lax.all_gather(v_weight[0], 'z', axis=0, tiled=True)  49.3 us
    all_to_all x1, blocking collectives, body(): diffs = exchange(ready)  18.4 us
    ppermute x4, starting transfers between devices, swaps(): lax.ppermute(a, 'yhi', [(0, 1), (1, 0)])  13.6 us
    pallas_call x6, Pallas kernels, local(): pl.pallas_call(kernel, out_shape=[jax.ShapeDtypeStruct(s, d) for s, d in...  9.81 us
    ppermute x1, starting transfers between devices, swaps(): lax.ppermute(a, ('core', 'z', 'yhi'), diagonal)  5.56 us
    all_to_all x1, starting transfers between devices, body(): diff = exchange(jnp.tile(diffs.reshape(16, 8, 512).sum(0), (16, 1)))  4.84 us
    ppermute x4, waiting for transfers between devices, swaps(): lax.ppermute(a, 'yhi', [(0, 1), (1, 0)])  4.68 us
    unnamed x14, local copies, waits for them, and re-layouts  4.43 us
  transfers between devices with their start and end apart: 9, of which 3 were waited for; matrix products, arithmetic and copies ran while one was open for 3% of the time, Pallas kernels for 6%

profile of v3, /device:TPU:24, one launch (start us, length us, event | category | flops | bytes accessed | tf_op | source)
XLA Modules:
  0.0 136.5 jit_solution(14687075821542613425)
XLA Ops:
  8.0 0.0 all-gather.3.cloned.1.call-start
  8.0 0.7 all-gather.3.cloned.1.call-update
  8.7 0.0 reduce-scatter.2.cloned.1.call-start
  8.8 0.1 pad_add_fusion.place
  8.9 1.2 copy-done.4
  10.1 0.9 copy-done.5
  11.0 0.9 pack.1
  11.9 0.0 copy-start.6
  11.9 0.7 copy-done.6
  12.6 3.1 %collective-permute-start = (bf16[128,1536]{1,0:T(8,128)(2,1)S(1)}, bf16[128,1536]{1,0:T(8,128)(2,1)S(1)}, u32[]{:S(2)}, u32[]{:S(2)}) collective-permute-start(bf16[128,1536]{1,0:T(8,128)(2,1)S(1)} %get-tuple-element.28), channel_id=1, source_target_pairs={{0,1},{1,0},{2,3},{3,2},{4,5},{5,4},{6,7},{7,6},{8,9},{9,8},{10,11... | collective-permute-start | bytes 1179656 | tf_op jit(solution)/shard_map/ppermute | solution.py:117
  15.7 5.6 %collective-permute-start.2 = (bf16[128,1536]{1,0:T(8,128)(2,1)S(1)}, bf16[128,1536]{1,0:T(8,128)(2,1)S(1)}, u32[]{:S(2)}, u32[]{:S(2)}) collective-permute-start(bf16[128,1536]{1,0:T(8,128)(2,1)S(1)} %get-tuple-element.30), channel_id=1, source_target_pairs={{0,3},{1,2},{2,1},{3,0},{4,7},{5,6},{6,5},{7,4},{8,11},{9,10},{10,... | collective-permute-start | bytes 1179656 | tf_op jit(solution)/shard_map/ppermute | solution.py:119
  21.3 2.0 %collective-permute-start.1 = (bf16[128,1536]{1,0:T(8,128)(2,1)S(1)}, bf16[128,1536]{1,0:T(8,128)(2,1)S(1)}, u32[]{:S(2)}, u32[]{:S(2)}) collective-permute-start(bf16[128,1536]{1,0:T(8,128)(2,1)S(1)} %get-tuple-element.29.own_more), channel_id=1, source_target_pairs={{0,2},{2,0},{4,6},{6,4},{8,10},{10,8},{12,14},{14,12},{16,18},{18,... | collective-permute-start | bytes 1179656 | tf_op jit(solution)/shard_map/ppermute | solution.py:118
  24.0 1.0 convert_subtract_fusion
  25.0 18.4 %all_to_all.20 = f32[16,8,512]{2,1,0:T(8,128)S(1)} all-to-all(f32[16,8,512]{2,1,0:T(8,128)S(1)} %bitcast.23), channel_id=1, replica_groups=mesh['ylo'=2,'x'=4,'core'=2,'z'=16,'yhi'=2] {'ylo','x','core'}, dimensions={0} | all-to-all | bytes 524288 | tf_op jit(solution)/shard_map/all_to_all | solution.py:135
  43.4 0.0 collective-permute-done.p1.other
  43.5 2.6 %weight_grad.1 = f32[1024,512]{1,0:T(8,128)} custom-call(s32[2]{0:T(128)S(1)} %pad_add_fusion.place, bf16[128,1536]{1,0:T(8,128)(2,1)S(1)} %get-tuple-element.27.p0.own, bf16[128,1536]{1,0:T(8,128)(2,1)S(1)} %collective-permute-done.p1.other, bf16[128,1536]{1,0:T(8,128)(2,1)S(1)} %collective-permute-done.1.p2, bf16[128,1536]{1,0:T(8,128)(2,1)S(1)} %collective-permute-done.2.p3), custom_call_target="tpu_custom_call" | custom-call | tf_op jit(solution)/shard_map/weight_grad/pallas_call | solution.py:20
  46.1 0.0 reduce-scatter.2.cloned.1.call-update
  46.1 0.7 tile.2
  46.9 4.8 %all-to-all-start.1 = ((f32[16,8,512]{2,1,0:T(8,128)}), f32[16,8,512]{2,1,0:T(8,128)S(1)}, u32[]{:S(2)}, u32[]{:S(2)}) async-start(f32[16,8,512]{2,1,0:T(8,128)} %tile.2), calls=%async_computation.1 | async-start | bytes 524288 | tf_op jit(solution)/shard_map/all_to_all | solution.py:145
  51.7 3.1 %collective-permute-start.3 = (bf16[128,1024]{1,0:T(8,128)(2,1)}, bf16[128,1024]{1,0:T(8,128)(2,1)}, u32[]{:S(2)}, u32[]{:S(2)}) collective-permute-start(bf16[128,1024]{1,0:T(8,128)(2,1)} %copy-done.6), channel_id=1, source_target_pairs={{0,1},{1,0},{2,3},{3,2},{4,5},{5,4},{6,7},{7,6},{8,9},{9,8},{10,11... | collective-permute-start | bytes 786440 | tf_op jit(solution)/shard_map/ppermute | solution.py:117
  54.8 3.4 %all-to-all-done.1 = f32[16,8,512]{2,1,0:T(8,128)S(1)} async-done(((f32[16,8,512]{2,1,0:T(8,128)}), f32[16,8,512]{2,1,0:T(8,128)S(1)}, u32[]{:S(2)}, u32[]{:S(2)}) %all-to-all-start.1) | async-done | bytes 262176 | tf_op jit(solution)/shard_map/all_to_all | solution.py:145
  58.2 1.5 %outer.2 = (f32[4,128,512]{2,1,0:T(8,128)}, f32[4,128,512]{2,1,0:T(8,128)}) custom-call(s32[1]{0:T(128)} %copy.12.chosen, f32[4,128,512]{2,1,0:T(8,128)S(1)} %copy-done.2, f32[4,128,512]{2,1,0:T(8,128)S(1)} %copy-done.3, f32[128,512]{1,0:T(8,128)S(1)} %bitcast.21), custom_call_target="tpu_custom_call" | custom-call | tf_op jit(solution)/shard_map/outer/pallas_call | solution.py:20
  59.7 49.3 %all-gather.3.cloned.1.call-done = bf16[1,2048,512]{2,1,0:T(8,128)(2,1)} async-done(((bf16[1,128,512]{2,1,0:T(8,128)(2,1)}), bf16[1,2048,512]{2,1,0:T(8,128)(2,1)}) %all-gather.3.cloned.1.call-update) | async-done | bytes 2097168 | tf_op jit(solution)/shard_map/all_gather | solution.py:127
  109.0 1.6 %copy-done = bf16[1,2048,512]{2,1,0:T(8,128)(2,1)S(1)} copy-done((bf16[1,2048,512]{2,1,0:T(8,128)(2,1)S(1)}, bf16[1,2048,512]{2,1,0:T(8,128)(2,1)}, u32[]{:S(2)}) %copy-start) | copy-done | bytes 2097176
  110.6 1.3 input_grad.1
  111.9 2.7 %collective-permute-start.5 = (bf16[128,2048]{1,0:T(8,128)(2,1)S(1)}, bf16[128,2048]{1,0:T(8,128)(2,1)S(1)}, u32[]{:S(2)}, u32[]{:S(2)}) collective-permute-start(bf16[128,2048]{1,0:T(8,128)(2,1)S(1)} %get-tuple-element.39), channel_id=1, source_target_pairs={{0,1},{1,0},{2,3},{3,2},{4,5},{5,4},{6,7},{7,6},{8,9},{9,8},{10,11... | collective-permute-start | bytes 1572872 | tf_op jit(solution)/shard_map/ppermute | solution.py:117
  114.6 1.7 %project.1 = (f32[128,512]{1,0:T(8,128)S(1)}, f32[128,512]{1,0:T(8,128)S(1)}) custom-call(s32[2]{0:T(128)S(1)} %pad_add_fusion.place, bf16[128,1536]{1,0:T(8,128)(2,1)S(1)} %get-tuple-element.27.p0.own, bf16[128,1536]{1,0:T(8,128)(2,1)S(1)} %get-tuple-element.29.own_more, bf16[128,1536]{1,0:T(8,128)(2,1)S(1)} %collective-permute-done.p1.other, ...), custom_call_target="tpu_custom_call" | custom-call | tf_op jit(solution)/shard_map/project/pallas_call | solution.py:20
  116.3 4.6 %collective-permute-start.4 = (f32[128,512]{1,0:T(8,128)S(1)}, f32[128,512]{1,0:T(8,128)S(1)}, u32[]{:S(2)}, u32[]{:S(2)}) collective-permute-start(f32[128,512]{1,0:T(8,128)S(1)} %get-tuple-element.37), channel_id=1, source_target_pairs={{0,1},{1,0},{2,3},{3,2},{4,5},{5,4},{6,7},{7,6},{8,9},{9,8},{10,11... | collective-permute-start | bytes 786440 | tf_op jit(solution)/shard_map/ppermute | solution.py:117
  120.9 0.0 reduce-scatter.2.cloned.1.call-done
  121.0 1.6 %fusion = bf16[1,128,512]{2,1,0:T(8,128)(2,1)} fusion(f32[128,512]{1,0:T(8,128)} %reduce-scatter.2.cloned.1.call-done), kind=kLoop, calls=%fused_computation.3 | loop fusion | flops 131072 | bytes 393216 | tf_op jit(solution)/shard_map/broadcast_in_dim | solution.py:141
  122.6 4.7 %collective-permute-done.4.v_other = f32[128,512]{1,0:T(8,128)S(1)} collective-permute-done((f32[128,512]{1,0:T(8,128)S(1)}, f32[128,512]{1,0:T(8,128)S(1)}, u32[]{:S(2)}, u32[]{:S(2)}) %collective-permute-start.4) | collective-permute-done | bytes 262176 | tf_op jit(solution)/shard_map/ppermute | solution.py:117
  127.3 1.8 %finish.1 = (bf16[128,512]{1,0:T(8,128)(2,1)}, bf16[128,4096]{1,0:T(8,128)(2,1)}) custom-call(s32[2]{0:T(128)S(1)} %pad_add_fusion.place, f32[128,512]{1,0:T(8,128)S(1)} %get-tuple-element.36.v_own, f32[128,512]{1,0:T(8,128)S(1)} %collective-permute-done.4.v_other, bf16[128,2048]{1,0:T(8,128)(2,1)S(1)} %get-tuple-element.38.g_own, ...), custom_call_target="tpu_custom_call" | custom-call | tf_op jit(solution)/shard_map/finish/pallas_call | solution.py:20
  (14 shorter events, 0.0 us)
Async XLA Ops:
  8.0 101.0 %all-gather.3.cloned.1.call-start = ((), (), s32[]{:S(2)}) async-start(), calls=%async_computation.4 | async-start | bytes 2228224 | tf_op jit(solution)/shard_map/all_gather | solution.py:127
  8.7 112.2 %reduce-scatter.2.cloned.1.call-start = ((), (), s32[]{:S(2)}) async-start(), calls=%async_computation.3 | async-start | bytes 2359296 | tf_op jit(solution)/shard_map/reduce_scatter | solution.py:140
  8.9 1.2 copy-start.4
  10.1 0.9 copy-start.5
  11.9 0.7 copy-start.6
  12.6 30.8 %collective-permute-start = (bf16[128,1536]{1,0:T(8,128)(2,1)S(1)}, bf16[128,1536]{1,0:T(8,128)(2,1)S(1)}, u32[]{:S(2)}, u32[]{:S(2)}) collective-permute-start(bf16[128,1536]{1,0:T(8,128)(2,1)S(1)} %get-tuple-element.28), channel_id=1, source_target_pairs={{0,1},{1,0},{2,3},{3,2},{4,5},{5,4},{6,7},{7,6},{8,9},{9,8},{10,11... | collective-permute-start | bytes 1179656 | tf_op jit(solution)/shard_map/ppermute | solution.py:117
  15.7 27.7 %collective-permute-start.2 = (bf16[128,1536]{1,0:T(8,128)(2,1)S(1)}, bf16[128,1536]{1,0:T(8,128)(2,1)S(1)}, u32[]{:S(2)}, u32[]{:S(2)}) collective-permute-start(bf16[128,1536]{1,0:T(8,128)(2,1)S(1)} %get-tuple-element.30), channel_id=1, source_target_pairs={{0,3},{1,2},{2,1},{3,0},{4,7},{5,6},{6,5},{7,4},{8,11},{9,10},{10,... | collective-permute-start | bytes 1179656 | tf_op jit(solution)/shard_map/ppermute | solution.py:119
  21.3 22.1 %collective-permute-start.1 = (bf16[128,1536]{1,0:T(8,128)(2,1)S(1)}, bf16[128,1536]{1,0:T(8,128)(2,1)S(1)}, u32[]{:S(2)}, u32[]{:S(2)}) collective-permute-start(bf16[128,1536]{1,0:T(8,128)(2,1)S(1)} %get-tuple-element.29.own_more), channel_id=1, source_target_pairs={{0,2},{2,0},{4,6},{6,4},{8,10},{10,8},{12,14},{14,12},{16,18},{18,... | collective-permute-start | bytes 1179656 | tf_op jit(solution)/shard_map/ppermute | solution.py:118
  46.1 12.1 %copy-start.2 = (f32[4,128,512]{2,1,0:T(8,128)S(1)}, f32[4,128,512]{2,1,0:T(8,128)}, u32[]{:S(2)}) copy-start(f32[4,128,512]{2,1,0:T(8,128)} %outer.3) | copy-start | bytes 3145732
  46.1 12.1 %copy-start.3 = (f32[4,128,512]{2,1,0:T(8,128)S(1)}, f32[4,128,512]{2,1,0:T(8,128)}, u32[]{:S(2)}) copy-start(f32[4,128,512]{2,1,0:T(8,128)} %momentum.1) | copy-start | bytes 3145732
  46.9 11.3 %all-to-all-start.1 = ((f32[16,8,512]{2,1,0:T(8,128)}), f32[16,8,512]{2,1,0:T(8,128)S(1)}, u32[]{:S(2)}, u32[]{:S(2)}) async-start(f32[16,8,512]{2,1,0:T(8,128)} %tile.2), calls=%async_computation.1 | async-start | bytes 524288 | tf_op jit(solution)/shard_map/all_to_all | solution.py:145
  51.7 62.9 %collective-permute-start.3 = (bf16[128,1024]{1,0:T(8,128)(2,1)}, bf16[128,1024]{1,0:T(8,128)(2,1)}, u32[]{:S(2)}, u32[]{:S(2)}) collective-permute-start(bf16[128,1024]{1,0:T(8,128)(2,1)} %copy-done.6), channel_id=1, source_target_pairs={{0,1},{1,0},{2,3},{3,2},{4,5},{5,4},{6,7},{7,6},{8,9},{9,8},{10,11... | collective-permute-start | bytes 786440 | tf_op jit(solution)/shard_map/ppermute | solution.py:117
  109.0 1.6 %copy-start = (bf16[1,2048,512]{2,1,0:T(8,128)(2,1)S(1)}, bf16[1,2048,512]{2,1,0:T(8,128)(2,1)}, u32[]{:S(2)}) copy-start(bf16[1,2048,512]{2,1,0:T(8,128)(2,1)} %all-gather.3.cloned.1.call-done) | copy-start | bytes 6291460
  110.6 4.0 %copy-start.1 = (bf16[1,2048,512]{2,1,0:T(8,128)(2,1)S(1)}, bf16[1,2048,512]{2,1,0:T(8,128)(2,1)}, u32[]{:S(2)}) copy-start(bf16[1,2048,512]{2,1,0:T(8,128)(2,1)} %all-gather.3.cloned.1.call-done) | copy-start | bytes 6291460
  111.9 15.4 %collective-permute-start.5 = (bf16[128,2048]{1,0:T(8,128)(2,1)S(1)}, bf16[128,2048]{1,0:T(8,128)(2,1)S(1)}, u32[]{:S(2)}, u32[]{:S(2)}) collective-permute-start(bf16[128,2048]{1,0:T(8,128)(2,1)S(1)} %get-tuple-element.39), channel_id=1, source_target_pairs={{0,1},{1,0},{2,3},{3,2},{4,5},{5,4},{6,7},{7,6},{8,9},{9,8},{10,11... | collective-permute-start | bytes 1572872 | tf_op jit(solution)/shard_map/ppermute | solution.py:117
  116.3 11.0 %collective-permute-start.4 = (f32[128,512]{1,0:T(8,128)S(1)}, f32[128,512]{1,0:T(8,128)S(1)}, u32[]{:S(2)}, u32[]{:S(2)}) collective-permute-start(f32[128,512]{1,0:T(8,128)S(1)} %get-tuple-element.37), channel_id=1, source_target_pairs={{0,1},{1,0},{2,3},{3,2},{4,5},{5,4},{6,7},{7,6},{8,9},{9,8},{10,11... | collective-permute-start | bytes 786440 | tf_op jit(solution)/shard_map/ppermute | solution.py:117
Sparse Core Ops, SparseCore 0:
  10.9 98.0 all-gather.2
Sparse Core Ops, SparseCore 1:
  46.2 70.8 reduce-scatter.1

commit v4 on v3

--- a/solution.py
+++ b/solution.py
@@ -134,14 +134,14 @@
     ready, *_ = lax.optimization_barrier((outer_now - snap.astype(F32), packed[0]))
     diffs = exchange(ready)
 
-    mine = lax.optimization_barrier((packs[0], diffs))[0]
+    more = swap[1](packed[4])
+    mine = lax.optimization_barrier((packs[0], diffs, more))[0]
     (partial,) = local(weight_grad_kernel, [((1024, 512), F32)], "weight_grad", (place, mine, *packs[1:]))
     rings = [[z_of for z_of in range(16) if z_of % 2 == odd] for odd in range(2)]
     summed = lax.psum_scatter(partial, "z", scatter_dimension=0, axis_index_groups=rings, tiled=True)
     weight_grad = (summed * (1.0 / math.sqrt(4096))).astype(BF16)[None]
 
-    more, diffs = lax.optimization_barrier((packed[4], diffs, partial))[:2]
-    more = swap[1](more)
+    diffs = lax.optimization_barrier((diffs, partial))[0]
     diff = exchange(jnp.tile(diffs.reshape(16, 8, 512).sum(0), (16, 1)))
     new_outer, new_momentum = local(
         outer_kernel, [((4, 128, 512), F32)] * 2, "outer", (frag_index, outer_params, momentum, diff)

time: 139 us -> 138 us (level)
  the two profiles are of different devices: /device:TPU:24 before, /device:TPU:4 now
where the time goes in v4:
time: 138 us; the launch traced here: 137 us
  waiting for transfers between devices  52.6 us (38%)
  blocking collectives  26.3 us (19%)
  starting transfers between devices  25.3 us (18%)
  between operations  16.3 us (12%)
  Pallas kernels  9.37 us (7%)
  other arithmetic  3.84 us (3%)
  local copies, waits for them, and re-layouts  3.76 us (3%)
    all_gather x1, waiting for transfers between devices, body(): gathered = lax.all_gather(v_weight[0], 'z', axis=0, tiled=True)  45.7 us
    ppermute x4, starting transfers between devices, swaps(): lax.ppermute(a, 'yhi', [(0, 1), (1, 0)])  19.4 us
    all_to_all x1, blocking collectives, body(): diffs = exchange(ready)  15.8 us
    all_to_all x1, blocking collectives, body(): diff = exchange(jnp.tile(diffs.reshape(16, 8, 512).sum(0), (16, 1)))  10.5 us
    pallas_call x6, Pallas kernels, local(): pl.pallas_call(kernel, out_shape=[jax.ShapeDtypeStruct(s, d) for s, d in...  9.37 us
    ppermute x4, waiting for transfers between devices, swaps(): lax.ppermute(a, 'yhi', [(0, 1), (1, 0)])  6.19 us
    unnamed x12, local copies, waits for them, and re-layouts  3.74 us
    ppermute x1, starting transfers between devices, swaps(): lax.ppermute(a, ('core', 'z', 'yhi'), diagonal)  3.6 us
  transfers between devices with their start and end apart: 8, of which 2 were waited for; matrix products, arithmetic and copies ran while one was open for 3% of the time, Pallas kernels for 5%

profile of v4, /device:TPU:4, one launch (start us, length us, event | category | flops | bytes accessed | tf_op | source)
XLA Modules:
  0.0 137.4 jit_solution(3771961342773067543)
XLA Ops:
  8.0 0.0 all-gather.3.cloned.1.call-start
  8.0 0.7 all-gather.3.cloned.1.call-update
  8.7 0.0 reduce-scatter.2.cloned.1.call-start
  8.8 0.1 pad_add_fusion.place
  8.9 1.2 copy-done.4
  10.1 0.9 copy-done.5
  11.0 0.9 pack.1
  11.9 5.1 %collective-permute-start.1 = (bf16[128,1536]{1,0:T(8,128)(2,1)S(1)}, bf16[128,1536]{1,0:T(8,128)(2,1)S(1)}, u32[]{:S(2)}, u32[]{:S(2)}) collective-permute-start(bf16[128,1536]{1,0:T(8,128)(2,1)S(1)} %get-tuple-element.27), channel_id=1, source_target_pairs={{0,1},{1,0},{2,3},{3,2},{4,5},{5,4},{6,7},{7,6},{8,9},{9,8},{10,11... | collective-permute-start | bytes 1179656 | tf_op jit(solution)/shard_map/ppermute | solution.py:117
  17.0 3.6 %collective-permute-start.3 = (bf16[128,1536]{1,0:T(8,128)(2,1)S(1)}, bf16[128,1536]{1,0:T(8,128)(2,1)S(1)}, u32[]{:S(2)}, u32[]{:S(2)}) collective-permute-start(bf16[128,1536]{1,0:T(8,128)(2,1)S(1)} %get-tuple-element.29), channel_id=1, source_target_pairs={{0,3},{1,2},{2,1},{3,0},{4,7},{5,6},{6,5},{7,4},{8,11},{9,10},{10,... | collective-permute-start | bytes 1179656 | tf_op jit(solution)/shard_map/ppermute | solution.py:119
  20.6 2.1 %collective-permute-start.2 = (bf16[128,1536]{1,0:T(8,128)(2,1)S(1)}, bf16[128,1536]{1,0:T(8,128)(2,1)S(1)}, u32[]{:S(2)}, u32[]{:S(2)}) collective-permute-start(bf16[128,1536]{1,0:T(8,128)(2,1)S(1)} %get-tuple-element.28.own_more), channel_id=1, source_target_pairs={{0,2},{2,0},{4,6},{6,4},{8,10},{10,8},{12,14},{14,12},{16,18},{18,... | collective-permute-start | bytes 1179656 | tf_op jit(solution)/shard_map/ppermute | solution.py:118
  22.8 5.0 %collective-permute-start = (bf16[128,1024]{1,0:T(8,128)(2,1)S(1)}, bf16[128,1024]{1,0:T(8,128)(2,1)S(1)}, u32[]{:S(2)}, u32[]{:S(2)}) collective-permute-start(bf16[128,1024]{1,0:T(8,128)(2,1)S(1)} %get-tuple-element.25), channel_id=1, source_target_pairs={{0,1},{1,0},{2,3},{3,2},{4,5},{5,4},{6,7},{7,6},{8,9},{9,8},{10,11... | collective-permute-start | bytes 786440 | tf_op jit(solution)/shard_map/ppermute | solution.py:117
  28.4 1.0 convert_subtract_fusion
  29.4 15.8 %all_to_all.20 = f32[16,8,512]{2,1,0:T(8,128)} all-to-all(f32[16,8,512]{2,1,0:T(8,128)S(1)} %bitcast.23), channel_id=1, replica_groups=mesh['ylo'=2,'x'=4,'core'=2,'z'=16,'yhi'=2] {'ylo','x','core'}, dimensions={0} | all-to-all | bytes 524288 | tf_op jit(solution)/shard_map/all_to_all | solution.py:135
  45.2 0.0 collective-permute-done.1.p1.other
  45.2 0.0 collective-permute-done.3.p3
  45.3 0.0 collective-permute-done.2.p2
  45.3 2.6 %weight_grad.1 = f32[1024,512]{1,0:T(8,128)} custom-call(s32[2]{0:T(128)S(1)} %pad_add_fusion.place, bf16[128,1536]{1,0:T(8,128)(2,1)S(1)} %get-tuple-element.26.p0.own, bf16[128,1536]{1,0:T(8,128)(2,1)S(1)} %collective-permute-done.1.p1.other, bf16[128,1536]{1,0:T(8,128)(2,1)S(1)} %collective-permute-done.2.p2, bf16[128,1536]{1,0:T(8,128)(2,1)S(1)} %collective-permute-done.3.p3), custom_call_target="tpu_custom_call" | custom-call | tf_op jit(solution)/shard_map/weight_grad/pallas_call | solution.py:20
  47.9 0.0 reduce-scatter.2.cloned.1.call-update
  47.9 1.1 bitcast_reduce_fusion
  49.0 10.5 %all_to_all.21 = f32[16,8,512]{2,1,0:T(8,128)S(1)} all-to-all(f32[16,8,512]{2,1,0:T(8,128)S(1)} %tile.2), channel_id=1, replica_groups=mesh['ylo'=2,'x'=4,'core'=2,'z'=16,'yhi'=2] {'ylo','x','core'}, dimensions={0} | all-to-all | bytes 524288 | tf_op jit(solution)/shard_map/all_to_all | solution.py:145
  59.5 1.5 %outer.2 = (f32[4,128,512]{2,1,0:T(8,128)}, f32[4,128,512]{2,1,0:T(8,128)}) custom-call(s32[1]{0:T(128)} %copy.12.chosen, f32[4,128,512]{2,1,0:T(8,128)S(1)} %copy-done.2, f32[4,128,512]{2,1,0:T(8,128)S(1)} %copy-done.3, f32[128,512]{1,0:T(8,128)S(1)} %bitcast.21), custom_call_target="tpu_custom_call" | custom-call | tf_op jit(solution)/shard_map/outer/pallas_call | solution.py:20
  61.1 45.7 %all-gather.3.cloned.1.call-done = bf16[1,2048,512]{2,1,0:T(8,128)(2,1)} async-done(((bf16[1,128,512]{2,1,0:T(8,128)(2,1)}), bf16[1,2048,512]{2,1,0:T(8,128)(2,1)}) %all-gather.3.cloned.1.call-update) | async-done | bytes 2097168 | tf_op jit(solution)/shard_map/all_gather | solution.py:127
  106.7 1.6 %copy-done = bf16[1,2048,512]{2,1,0:T(8,128)(2,1)S(1)} copy-done((bf16[1,2048,512]{2,1,0:T(8,128)(2,1)S(1)}, bf16[1,2048,512]{2,1,0:T(8,128)(2,1)}, u32[]{:S(2)}) %copy-start) | copy-done | bytes 2097176
  108.3 1.3 input_grad.1
  109.6 7.5 %collective-permute-start.5 = (bf16[128,2048]{1,0:T(8,128)(2,1)S(1)}, bf16[128,2048]{1,0:T(8,128)(2,1)S(1)}, u32[]{:S(2)}, u32[]{:S(2)}) collective-permute-start(bf16[128,2048]{1,0:T(8,128)(2,1)S(1)} %get-tuple-element.37), channel_id=1, source_target_pairs={{0,1},{1,0},{2,3},{3,2},{4,5},{5,4},{6,7},{7,6},{8,9},{9,8},{10,11... | collective-permute-start | bytes 1572872 | tf_op jit(solution)/shard_map/ppermute | solution.py:117
  117.1 1.2 project.1
  118.3 1.9 %collective-permute-start.4 = (f32[128,512]{1,0:T(8,128)S(1)}, f32[128,512]{1,0:T(8,128)S(1)}, u32[]{:S(2)}, u32[]{:S(2)}) collective-permute-start(f32[128,512]{1,0:T(8,128)S(1)} %get-tuple-element.35), channel_id=1, source_target_pairs={{0,1},{1,0},{2,3},{3,2},{4,5},{5,4},{6,7},{7,6},{8,9},{9,8},{10,11... | collective-permute-start | bytes 786440 | tf_op jit(solution)/shard_map/ppermute | solution.py:117
  120.3 0.0 reduce-scatter.2.cloned.1.call-done
  120.3 1.6 %fusion = bf16[1,128,512]{2,1,0:T(8,128)(2,1)} fusion(f32[128,512]{1,0:T(8,128)} %reduce-scatter.2.cloned.1.call-done), kind=kLoop, calls=%fused_computation.3 | loop fusion | flops 131072 | bytes 393216 | tf_op jit(solution)/shard_map/broadcast_in_dim | solution.py:142
  121.9 6.2 %collective-permute-done.4.v_other = f32[128,512]{1,0:T(8,128)S(1)} collective-permute-done((f32[128,512]{1,0:T(8,128)S(1)}, f32[128,512]{1,0:T(8,128)S(1)}, u32[]{:S(2)}, u32[]{:S(2)}) %collective-permute-start.4) | collective-permute-done | bytes 262176 | tf_op jit(solution)/shard_map/ppermute | solution.py:117
  128.1 0.0 collective-permute-done.5.g_other
  128.1 1.8 %finish.1 = (bf16[128,512]{1,0:T(8,128)(2,1)}, bf16[128,4096]{1,0:T(8,128)(2,1)}) custom-call(s32[2]{0:T(128)S(1)} %pad_add_fusion.place, f32[128,512]{1,0:T(8,128)S(1)} %get-tuple-element.34.v_own, f32[128,512]{1,0:T(8,128)S(1)} %collective-permute-done.4.v_other, bf16[128,2048]{1,0:T(8,128)(2,1)S(1)} %get-tuple-element.36.g_own, ...), custom_call_target="tpu_custom_call" | custom-call | tf_op jit(solution)/shard_map/finish/pallas_call | solution.py:20
  (11 shorter events, 0.0 us)
Async XLA Ops:
  8.0 98.7 %all-gather.3.cloned.1.call-start = ((), (), s32[]{:S(2)}) async-start(), calls=%async_computation.4 | async-start | bytes 2228224 | tf_op jit(solution)/shard_map/all_gather | solution.py:127
  8.7 111.6 %reduce-scatter.2.cloned.1.call-start = ((), (), s32[]{:S(2)}) async-start(), calls=%async_computation.3 | async-start | bytes 2359296 | tf_op jit(solution)/shard_map/reduce_scatter | solution.py:141
  8.9 1.2 copy-start.4
  10.1 0.9 copy-start.5
  11.9 33.4 %collective-permute-start.1 = (bf16[128,1536]{1,0:T(8,128)(2,1)S(1)}, bf16[128,1536]{1,0:T(8,128)(2,1)S(1)}, u32[]{:S(2)}, u32[]{:S(2)}) collective-permute-start(bf16[128,1536]{1,0:T(8,128)(2,1)S(1)} %get-tuple-element.27), channel_id=1, source_target_pairs={{0,1},{1,0},{2,3},{3,2},{4,5},{5,4},{6,7},{7,6},{8,9},{9,8},{10,11... | collective-permute-start | bytes 1179656 | tf_op jit(solution)/shard_map/ppermute | solution.py:117
  17.0 28.2 %collective-permute-start.3 = (bf16[128,1536]{1,0:T(8,128)(2,1)S(1)}, bf16[128,1536]{1,0:T(8,128)(2,1)S(1)}, u32[]{:S(2)}, u32[]{:S(2)}) collective-permute-start(bf16[128,1536]{1,0:T(8,128)(2,1)S(1)} %get-tuple-element.29), channel_id=1, source_target_pairs={{0,3},{1,2},{2,1},{3,0},{4,7},{5,6},{6,5},{7,4},{8,11},{9,10},{10,... | collective-permute-start | bytes 1179656 | tf_op jit(solution)/shard_map/ppermute | solution.py:119
  20.6 24.6 %collective-permute-start.2 = (bf16[128,1536]{1,0:T(8,128)(2,1)S(1)}, bf16[128,1536]{1,0:T(8,128)(2,1)S(1)}, u32[]{:S(2)}, u32[]{:S(2)}) collective-permute-start(bf16[128,1536]{1,0:T(8,128)(2,1)S(1)} %get-tuple-element.28.own_more), channel_id=1, source_target_pairs={{0,2},{2,0},{4,6},{6,4},{8,10},{10,8},{12,14},{14,12},{16,18},{18,... | collective-permute-start | bytes 1179656 | tf_op jit(solution)/shard_map/ppermute | solution.py:118
  22.8 22.5 %collective-permute-start = (bf16[128,1024]{1,0:T(8,128)(2,1)S(1)}, bf16[128,1024]{1,0:T(8,128)(2,1)S(1)}, u32[]{:S(2)}, u32[]{:S(2)}) collective-permute-start(bf16[128,1024]{1,0:T(8,128)(2,1)S(1)} %get-tuple-element.25), channel_id=1, source_target_pairs={{0,1},{1,0},{2,3},{3,2},{4,5},{5,4},{6,7},{7,6},{8,9},{9,8},{10,11... | collective-permute-start | bytes 786440 | tf_op jit(solution)/shard_map/ppermute | solution.py:117
  47.9 11.7 %copy-start.2 = (f32[4,128,512]{2,1,0:T(8,128)S(1)}, f32[4,128,512]{2,1,0:T(8,128)}, u32[]{:S(2)}) copy-start(f32[4,128,512]{2,1,0:T(8,128)} %outer.3) | copy-start | bytes 3145732
  47.9 11.7 %copy-start.3 = (f32[4,128,512]{2,1,0:T(8,128)S(1)}, f32[4,128,512]{2,1,0:T(8,128)}, u32[]{:S(2)}) copy-start(f32[4,128,512]{2,1,0:T(8,128)} %momentum.1) | copy-start | bytes 3145732
  106.7 1.6 %copy-start = (bf16[1,2048,512]{2,1,0:T(8,128)(2,1)S(1)}, bf16[1,2048,512]{2,1,0:T(8,128)(2,1)}, u32[]{:S(2)}) copy-start(bf16[1,2048,512]{2,1,0:T(8,128)(2,1)} %all-gather.3.cloned.1.call-done) | copy-start | bytes 6291460
  108.3 8.8 %copy-start.1 = (bf16[1,2048,512]{2,1,0:T(8,128)(2,1)S(1)}, bf16[1,2048,512]{2,1,0:T(8,128)(2,1)}, u32[]{:S(2)}) copy-start(bf16[1,2048,512]{2,1,0:T(8,128)(2,1)} %all-gather.3.cloned.1.call-done) | copy-start | bytes 6291460
  109.6 18.5 %collective-permute-start.5 = (bf16[128,2048]{1,0:T(8,128)(2,1)S(1)}, bf16[128,2048]{1,0:T(8,128)(2,1)S(1)}, u32[]{:S(2)}, u32[]{:S(2)}) collective-permute-start(bf16[128,2048]{1,0:T(8,128)(2,1)S(1)} %get-tuple-element.37), channel_id=1, source_target_pairs={{0,1},{1,0},{2,3},{3,2},{4,5},{5,4},{6,7},{7,6},{8,9},{9,8},{10,11... | collective-permute-start | bytes 1572872 | tf_op jit(solution)/shard_map/ppermute | solution.py:117
  118.3 9.8 %collective-permute-start.4 = (f32[128,512]{1,0:T(8,128)S(1)}, f32[128,512]{1,0:T(8,128)S(1)}, u32[]{:S(2)}, u32[]{:S(2)}) collective-permute-start(f32[128,512]{1,0:T(8,128)S(1)} %get-tuple-element.35), channel_id=1, source_target_pairs={{0,1},{1,0},{2,3},{3,2},{4,5},{5,4},{6,7},{7,6},{8,9},{9,8},{10,11... | collective-permute-start | bytes 786440 | tf_op jit(solution)/shard_map/ppermute | solution.py:117
Sparse Core Ops, SparseCore 0:
  10.9 95.7 all-gather.2
Sparse Core Ops, SparseCore 1:
  48.0 69.7 reduce-scatter.1

commit v5 on v4

--- a/solution.py
+++ b/solution.py
@@ -132,7 +132,7 @@
     outer_now = lax.dynamic_index_in_dim(outer_params, frag_index[0], 0, keepdims=False)
     snap = lax.dynamic_index_in_dim(snapshot[0], frag_index[0], 0, keepdims=False)
     ready, *_ = lax.optimization_barrier((outer_now - snap.astype(F32), packed[0]))
-    diffs = exchange(ready)
+    diffs = jnp.tile(exchange(ready).reshape(16, 8, 512).sum(0), (16, 1))
 
     more = swap[1](packed[4])
     mine = lax.optimization_barrier((packs[0], diffs, more))[0]
@@ -142,7 +142,7 @@
     weight_grad = (summed * (1.0 / math.sqrt(4096))).astype(BF16)[None]
 
     diffs = lax.optimization_barrier((diffs, partial))[0]
-    diff = exchange(jnp.tile(diffs.reshape(16, 8, 512).sum(0), (16, 1)))
+    diff = exchange(diffs)
     new_outer, new_momentum = local(
         outer_kernel, [((4, 128, 512), F32)] * 2, "outer", (frag_index, outer_params, momentum, diff)
     )

time: 138 us -> 135 us (0.978)
  the two profiles are of different devices: /device:TPU:4 before, /device:TPU:24 now
where the time goes in v5:
time: 135 us
  waiting for transfers between devices  57.7 us (43%)
  starting transfers between devices  30.5 us (23%)
  between operations  16.2 us (12%)
  blocking collectives  11.5 us (9%)
  Pallas kernels  9.4 us (7%)
  local copies, waits for them, and re-layouts  5.18 us (4%)
  other arithmetic  4.05 us (3%)
    all_gather x1, waiting for transfers between devices, body(): gathered = lax.all_gather(v_weight[0], 'z', axis=0, tiled=True)  36.4 us
    ppermute x4, starting transfers between devices, swaps(): lax.ppermute(a, 'yhi', [(0, 1), (1, 0)])  19.3 us
    ppermute x4, waiting for transfers between devices, swaps(): lax.ppermute(a, 'yhi', [(0, 1), (1, 0)])  12.6 us
    all_to_all x1, blocking collectives, body(): diff = exchange(diffs)  11.5 us
    pallas_call x6, Pallas kernels, local(): pl.pallas_call(kernel, out_shape=[jax.ShapeDtypeStruct(s, d) for s, d in...  9.4 us
    reduce_scatter x1, waiting for transfers between devices, body(): lax.psum_scatter(partial, 'z', scatter_dimension=0, axis_index_groups=rin...  8.09 us
    all_to_all x1, starting transfers between devices, body(): diffs = jnp.tile(exchange(ready).reshape(16, 8, 512).sum(0), (16, 1))  5.78 us
    unnamed x12, local copies, waits for them, and re-layouts  3.73 us
  transfers between devices with their start and end apart: 9, of which 3 were waited for; matrix products, arithmetic and copies ran while one was open for 4% of the time, Pallas kernels for 6%

profile of v5, /device:TPU:24, one launch (start us, length us, event | category | flops | bytes accessed | tf_op | source)
XLA Modules:
  0.0 134.6 jit_solution(3038580754695647405)
XLA Ops:
  8.0 0.0 all-gather.3.cloned.1.call-start
  8.0 0.7 all-gather.3.cloned.1.call-update
  9.4 0.1 pad_add_fusion.place
  9.5 1.2 copy-done.4
  10.7 0.9 copy-done.5
  11.6 0.9 pack.1
  12.5 1.7 %convert_subtract_fusion = f32[128,512]{1,0:T(8,128)} fusion(f32[4,128,512]{2,1,0:T(8,128)} %outer.3, s32[]{:T(128)S(6)} %select_n.6, bf16[1,4,128,512]{3,2,1,0:T(8,128)(2,1)} %param.12), kind=kLoop, calls=%fused_computation | loop fusion | flops 131072 | bytes 655364 | tf_op jit(solution)/shard_map/sub | solution.py:134
  14.2 5.8 %all-to-all-start = ((f32[16,8,512]{2,1,0:T(8,128)}), f32[16,8,512]{2,1,0:T(8,128)S(1)}, u32[]{:S(2)}, u32[]{:S(2)}) async-start(f32[16,8,512]{2,1,0:T(8,128)} %bitcast.5), calls=%async_computation | async-start | bytes 524288 | tf_op jit(solution)/shard_map/all_to_all | solution.py:135
  20.0 0.0 reduce-scatter.2.cloned.1.call-start
  20.0 6.6 %collective-permute-start.1 = (bf16[128,1536]{1,0:T(8,128)(2,1)S(1)}, bf16[128,1536]{1,0:T(8,128)(2,1)S(1)}, u32[]{:S(2)}, u32[]{:S(2)}) collective-permute-start(bf16[128,1536]{1,0:T(8,128)(2,1)S(1)} %get-tuple-element.27), channel_id=1, source_target_pairs={{0,1},{1,0},{2,3},{3,2},{4,5},{5,4},{6,7},{7,6},{8,9},{9,8},{10,11... | collective-permute-start | bytes 1179656 | tf_op jit(solution)/shard_map/ppermute | solution.py:117
  26.6 2.1 %collective-permute-start.3 = (bf16[128,1536]{1,0:T(8,128)(2,1)S(1)}, bf16[128,1536]{1,0:T(8,128)(2,1)S(1)}, u32[]{:S(2)}, u32[]{:S(2)}) collective-permute-start(bf16[128,1536]{1,0:T(8,128)(2,1)S(1)} %get-tuple-element.29), channel_id=1, source_target_pairs={{0,3},{1,2},{2,1},{3,0},{4,7},{5,6},{6,5},{7,4},{8,11},{9,10},{10,... | collective-permute-start | bytes 1179656 | tf_op jit(solution)/shard_map/ppermute | solution.py:119
  28.8 3.2 %collective-permute-start.2 = (bf16[128,1536]{1,0:T(8,128)(2,1)S(1)}, bf16[128,1536]{1,0:T(8,128)(2,1)S(1)}, u32[]{:S(2)}, u32[]{:S(2)}) collective-permute-start(bf16[128,1536]{1,0:T(8,128)(2,1)S(1)} %get-tuple-element.28.own_more), channel_id=1, source_target_pairs={{0,2},{2,0},{4,6},{6,4},{8,10},{10,8},{12,14},{14,12},{16,18},{18,... | collective-permute-start | bytes 1179656 | tf_op jit(solution)/shard_map/ppermute | solution.py:118
  31.9 5.4 %collective-permute-start = (bf16[128,1024]{1,0:T(8,128)(2,1)S(1)}, bf16[128,1024]{1,0:T(8,128)(2,1)S(1)}, u32[]{:S(2)}, u32[]{:S(2)}) collective-permute-start(bf16[128,1024]{1,0:T(8,128)(2,1)S(1)} %get-tuple-element.25), channel_id=1, source_target_pairs={{0,1},{1,0},{2,3},{3,2},{4,5},{5,4},{6,7},{7,6},{8,9},{9,8},{10,11... | collective-permute-start | bytes 786440 | tf_op jit(solution)/shard_map/ppermute | solution.py:117
  37.4 0.0 all-to-all-done
  37.4 0.6 reduce_sum.9
  38.0 1.4 %broadcast_bitcast_fusion = f32[128,512]{1,0:T(8,128)} fusion(f32[8,512]{1,0:T(8,128)} %reduce_sum.9), kind=kLoop, calls=%fused_computation.3 | loop fusion | bytes 278528 | tf_op jit(solution)/shard_map/tile | solution.py:135
  39.4 12.6 %collective-permute-done.other_more = bf16[128,1024]{1,0:T(8,128)(2,1)S(1)} collective-permute-done((bf16[128,1024]{1,0:T(8,128)(2,1)S(1)}, bf16[128,1024]{1,0:T(8,128)(2,1)S(1)}, u32[]{:S(2)}, u32[]{:S(2)}) %collective-permute-start) | collective-permute-done | bytes 262176 | tf_op jit(solution)/shard_map/ppermute | solution.py:117
  52.0 0.0 collective-permute-done.1.p1.other
  52.0 0.0 collective-permute-done.3.p3
  52.0 2.6 %weight_grad.1 = f32[1024,512]{1,0:T(8,128)} custom-call(s32[2]{0:T(128)S(1)} %pad_add_fusion.place, bf16[128,1536]{1,0:T(8,128)(2,1)S(1)} %get-tuple-element.26.p0.own, bf16[128,1536]{1,0:T(8,128)(2,1)S(1)} %collective-permute-done.1.p1.other, bf16[128,1536]{1,0:T(8,128)(2,1)S(1)} %collective-permute-done.2.p2, bf16[128,1536]{1,0:T(8,128)(2,1)S(1)} %collective-permute-done.3.p3), custom_call_target="tpu_custom_call" | custom-call | tf_op jit(solution)/shard_map/weight_grad/pallas_call | solution.py:20
  54.6 0.0 reduce-scatter.2.cloned.1.call-update
  54.6 11.5 %all_to_all.20 = f32[16,8,512]{2,1,0:T(8,128)S(1)} all-to-all(f32[16,8,512]{2,1,0:T(8,128)} %bitcast.22), channel_id=1, replica_groups=mesh['ylo'=2,'x'=4,'core'=2,'z'=16,'yhi'=2] {'ylo','x','core'}, dimensions={0} | all-to-all | bytes 524288 | tf_op jit(solution)/shard_map/all_to_all | solution.py:145
  66.2 1.5 %outer.2 = (f32[4,128,512]{2,1,0:T(8,128)}, f32[4,128,512]{2,1,0:T(8,128)}) custom-call(s32[1]{0:T(128)} %copy.12.chosen, f32[4,128,512]{2,1,0:T(8,128)S(1)} %copy-done.2, f32[4,128,512]{2,1,0:T(8,128)S(1)} %copy-done.3, f32[128,512]{1,0:T(8,128)S(1)} %bitcast.21), custom_call_target="tpu_custom_call" | custom-call | tf_op jit(solution)/shard_map/outer/pallas_call | solution.py:20
  67.7 36.4 %all-gather.3.cloned.1.call-done = bf16[1,2048,512]{2,1,0:T(8,128)(2,1)} async-done(((bf16[1,128,512]{2,1,0:T(8,128)(2,1)}), bf16[1,2048,512]{2,1,0:T(8,128)(2,1)}) %all-gather.3.cloned.1.call-update) | async-done | bytes 2097168 | tf_op jit(solution)/shard_map/all_gather | solution.py:127
  104.1 1.6 %copy-done = bf16[1,2048,512]{2,1,0:T(8,128)(2,1)S(1)} copy-done((bf16[1,2048,512]{2,1,0:T(8,128)(2,1)S(1)}, bf16[1,2048,512]{2,1,0:T(8,128)(2,1)}, u32[]{:S(2)}) %copy-start) | copy-done | bytes 2097176
  105.7 1.3 input_grad.1
  107.0 4.4 %collective-permute-start.5 = (bf16[128,2048]{1,0:T(8,128)(2,1)S(1)}, bf16[128,2048]{1,0:T(8,128)(2,1)S(1)}, u32[]{:S(2)}, u32[]{:S(2)}) collective-permute-start(bf16[128,2048]{1,0:T(8,128)(2,1)S(1)} %get-tuple-element.37), channel_id=1, source_target_pairs={{0,1},{1,0},{2,3},{3,2},{4,5},{5,4},{6,7},{7,6},{8,9},{9,8},{10,11... | collective-permute-start | bytes 1572872 | tf_op jit(solution)/shard_map/ppermute | solution.py:117
  111.4 1.2 project.1
  112.6 3.0 %collective-permute-start.4 = (f32[128,512]{1,0:T(8,128)S(1)}, f32[128,512]{1,0:T(8,128)S(1)}, u32[]{:S(2)}, u32[]{:S(2)}) collective-permute-start(f32[128,512]{1,0:T(8,128)S(1)} %get-tuple-element.35), channel_id=1, source_target_pairs={{0,1},{1,0},{2,3},{3,2},{4,5},{5,4},{6,7},{7,6},{8,9},{9,8},{10,11... | collective-permute-start | bytes 786440 | tf_op jit(solution)/shard_map/ppermute | solution.py:117
  115.6 8.1 %reduce-scatter.2.cloned.1.call-done = f32[128,512]{1,0:T(8,128)} async-done(((f32[1024,512]{1,0:T(8,128)}), f32[128,512]{1,0:T(8,128)}) %reduce-scatter.2.cloned.1.call-update) | async-done | bytes 262160 | tf_op jit(solution)/shard_map/reduce_scatter | solution.py:141
  123.7 1.6 %fusion = bf16[1,128,512]{2,1,0:T(8,128)(2,1)} fusion(f32[128,512]{1,0:T(8,128)} %reduce-scatter.2.cloned.1.call-done), kind=kLoop, calls=%fused_computation.2 | loop fusion | flops 131072 | bytes 393216 | tf_op jit(solution)/shard_map/broadcast_in_dim | solution.py:142
  125.3 1.8 %finish.1 = (bf16[128,512]{1,0:T(8,128)(2,1)}, bf16[128,4096]{1,0:T(8,128)(2,1)}) custom-call(s32[2]{0:T(128)S(1)} %pad_add_fusion.place, f32[128,512]{1,0:T(8,128)S(1)} %get-tuple-element.34.v_own, f32[128,512]{1,0:T(8,128)S(1)} %collective-permute-done.4.v_other, bf16[128,2048]{1,0:T(8,128)(2,1)S(1)} %get-tuple-element.36.g_own, ...), custom_call_target="tpu_custom_call" | custom-call | tf_op jit(solution)/shard_map/finish/pallas_call | solution.py:20
  (12 shorter events, 0.0 us)
Async XLA Ops:
  8.0 96.1 %all-gather.3.cloned.1.call-start = ((), (), s32[]{:S(2)}) async-start(), calls=%async_computation.4 | async-start | bytes 2228224 | tf_op jit(solution)/shard_map/all_gather | solution.py:127
  9.5 1.2 copy-start.4
  10.7 0.9 copy-start.5
  14.2 23.1 %all-to-all-start = ((f32[16,8,512]{2,1,0:T(8,128)}), f32[16,8,512]{2,1,0:T(8,128)S(1)}, u32[]{:S(2)}, u32[]{:S(2)}) async-start(f32[16,8,512]{2,1,0:T(8,128)} %bitcast.5), calls=%async_computation | async-start | bytes 524288 | tf_op jit(solution)/shard_map/all_to_all | solution.py:135
  20.0 103.7 %reduce-scatter.2.cloned.1.call-start = ((), (), s32[]{:S(2)}) async-start(), calls=%async_computation.3 | async-start | bytes 2359296 | tf_op jit(solution)/shard_map/reduce_scatter | solution.py:141
  20.0 32.0 %collective-permute-start.1 = (bf16[128,1536]{1,0:T(8,128)(2,1)S(1)}, bf16[128,1536]{1,0:T(8,128)(2,1)S(1)}, u32[]{:S(2)}, u32[]{:S(2)}) collective-permute-start(bf16[128,1536]{1,0:T(8,128)(2,1)S(1)} %get-tuple-element.27), channel_id=1, source_target_pairs={{0,1},{1,0},{2,3},{3,2},{4,5},{5,4},{6,7},{7,6},{8,9},{9,8},{10,11... | collective-permute-start | bytes 1179656 | tf_op jit(solution)/shard_map/ppermute | solution.py:117
  26.6 25.4 %collective-permute-start.3 = (bf16[128,1536]{1,0:T(8,128)(2,1)S(1)}, bf16[128,1536]{1,0:T(8,128)(2,1)S(1)}, u32[]{:S(2)}, u32[]{:S(2)}) collective-permute-start(bf16[128,1536]{1,0:T(8,128)(2,1)S(1)} %get-tuple-element.29), channel_id=1, source_target_pairs={{0,3},{1,2},{2,1},{3,0},{4,7},{5,6},{6,5},{7,4},{8,11},{9,10},{10,... | collective-permute-start | bytes 1179656 | tf_op jit(solution)/shard_map/ppermute | solution.py:119
  28.8 23.2 %collective-permute-start.2 = (bf16[128,1536]{1,0:T(8,128)(2,1)S(1)}, bf16[128,1536]{1,0:T(8,128)(2,1)S(1)}, u32[]{:S(2)}, u32[]{:S(2)}) collective-permute-start(bf16[128,1536]{1,0:T(8,128)(2,1)S(1)} %get-tuple-element.28.own_more), channel_id=1, source_target_pairs={{0,2},{2,0},{4,6},{6,4},{8,10},{10,8},{12,14},{14,12},{16,18},{18,... | collective-permute-start | bytes 1179656 | tf_op jit(solution)/shard_map/ppermute | solution.py:118
  31.9 20.1 %collective-permute-start = (bf16[128,1024]{1,0:T(8,128)(2,1)S(1)}, bf16[128,1024]{1,0:T(8,128)(2,1)S(1)}, u32[]{:S(2)}, u32[]{:S(2)}) collective-permute-start(bf16[128,1024]{1,0:T(8,128)(2,1)S(1)} %get-tuple-element.25), channel_id=1, source_target_pairs={{0,1},{1,0},{2,3},{3,2},{4,5},{5,4},{6,7},{7,6},{8,9},{9,8},{10,11... | collective-permute-start | bytes 786440 | tf_op jit(solution)/shard_map/ppermute | solution.py:117
  54.6 11.6 %copy-start.2 = (f32[4,128,512]{2,1,0:T(8,128)S(1)}, f32[4,128,512]{2,1,0:T(8,128)}, u32[]{:S(2)}) copy-start(f32[4,128,512]{2,1,0:T(8,128)} %outer.3) | copy-start | bytes 3145732
  54.6 11.6 %copy-start.3 = (f32[4,128,512]{2,1,0:T(8,128)S(1)}, f32[4,128,512]{2,1,0:T(8,128)}, u32[]{:S(2)}) copy-start(f32[4,128,512]{2,1,0:T(8,128)} %momentum.1) | copy-start | bytes 3145732
  104.1 1.6 %copy-start = (bf16[1,2048,512]{2,1,0:T(8,128)(2,1)S(1)}, bf16[1,2048,512]{2,1,0:T(8,128)(2,1)}, u32[]{:S(2)}) copy-start(bf16[1,2048,512]{2,1,0:T(8,128)(2,1)} %all-gather.3.cloned.1.call-done) | copy-start | bytes 6291460
  105.7 5.7 %copy-start.1 = (bf16[1,2048,512]{2,1,0:T(8,128)(2,1)S(1)}, bf16[1,2048,512]{2,1,0:T(8,128)(2,1)}, u32[]{:S(2)}) copy-start(bf16[1,2048,512]{2,1,0:T(8,128)(2,1)} %all-gather.3.cloned.1.call-done) | copy-start | bytes 6291460
  107.0 18.3 %collective-permute-start.5 = (bf16[128,2048]{1,0:T(8,128)(2,1)S(1)}, bf16[128,2048]{1,0:T(8,128)(2,1)S(1)}, u32[]{:S(2)}, u32[]{:S(2)}) collective-permute-start(bf16[128,2048]{1,0:T(8,128)(2,1)S(1)} %get-tuple-element.37), channel_id=1, source_target_pairs={{0,1},{1,0},{2,3},{3,2},{4,5},{5,4},{6,7},{7,6},{8,9},{9,8},{10,11... | collective-permute-start | bytes 1572872 | tf_op jit(solution)/shard_map/ppermute | solution.py:117
  112.6 12.7 %collective-permute-start.4 = (f32[128,512]{1,0:T(8,128)S(1)}, f32[128,512]{1,0:T(8,128)S(1)}, u32[]{:S(2)}, u32[]{:S(2)}) collective-permute-start(f32[128,512]{1,0:T(8,128)S(1)} %get-tuple-element.35), channel_id=1, source_target_pairs={{0,1},{1,0},{2,3},{3,2},{4,5},{5,4},{6,7},{7,6},{8,9},{9,8},{10,11... | collective-permute-start | bytes 786440 | tf_op jit(solution)/shard_map/ppermute | solution.py:117
Sparse Core Ops, SparseCore 0:
  10.9 93.1 all-gather.2
Sparse Core Ops, SparseCore 1:
  54.7 68.9 reduce-scatter.1
